TPU v7x, 256 devices: a whole 4x4x8 slice. The times are simulated.
256 devices in a mesh: section: 4 (over z_lo, core), seq: 64 (over y, x, z_hi).
Axes of the slice: x: 4, y: 4, z: 8 (z_hi: 4, z_lo: 2; z = z_hi * 2 + z_lo), core: 2. Of those that a mesh axis runs over, the one named last changes fastest.
Arguments:
- acts_in: bfloat16 [4, 8192, 4096], P('section', 'seq'), may hold values from -8 to 8
- first_in: bfloat16 [8192, 4096], P('seq'), may hold values from -8 to 8
- saved_one: bfloat16 [4, 8192, 4096], P('section', 'seq'), may hold values from -8 to 8
- cot_one: bfloat16 [4, 8192, 4096], P('section', 'seq'), may hold values from -6 to 6
- saved_two: bfloat16 [4, 8192, 4096], P('section', 'seq'), may hold values from -8 to 8
- cot_last: bfloat16 [8192, 4096], P('seq'), may hold values from -6 to 6
- gains: float32 [4, 3, 4096], P('section'), may hold values from 0.1 to 1.9
- slopes: float32 [4, 32], P('section'), may hold values from 0.003 to 0.5
- ocean: int32 [8192], replicated, may hold values from 0 to 1, as said below
- places: int32 [2, 8192], replicated, may hold values from 0 to 63
Outputs:
- out_one: bfloat16 [4, 8192, 4096], P('section', 'seq')
- grad_one: bfloat16 [4, 8192, 4096], P('section', 'seq')
- fwd_two: bfloat16 [4, 8192, 4096], P('section', 'seq')
- bwd_two: bfloat16 [4, 8192, 4096], P('section', 'seq')
- gain_grads: float32 [4, 3, 4096], P('section')
Inputs may be any that keep to these rules, and one draw needn't show every extreme that they name: The first patch of every region of 256 patches is ocean.
All inputs are finite; a program needn't handle non-finite values.
Results may differ from a plain program's by a relative error of at most 0.034.
Values may be sent and summed in bfloat16 or wider, within the bound.
No kernel may reach another device: no remote copies, remote signals or barrier semaphores. Data moves between devices by JAX's collectives and lax.ppermute only.
A program may use at most 192 MiB of HBM per device.

v0:
```python
import jax
import jax.numpy as jnp
from jax import lax
from jax.sharding import PartitionSpec as P

D = 4096
HEADS = 32
HD = 128
REGION = 256


def shifted(value, axis, steps):
    count = lax.axis_size(axis)
    initial, last = (max(0, -steps), min(count, count - steps))
    return lax.ppermute(value, axis, [(source, source + steps) for source in range(initial, last)])


def normed(hidden_wide):
    return hidden_wide * lax.rsqrt(
        jnp.mean(hidden_wide * hidden_wide, axis=-1, keepdims=True) + 1e-05
    )


def product(einsum_form, left, right):
    return jnp.einsum(einsum_form, left, right, preferred_element_type=jnp.float32)


def score_table(query_b, key_b, query_pos, key_pos, key_ocean, slope_vec):
    scores = product("bmhe,blhe->bhml", query_b, key_b) * query_b.shape[-1] ** (-0.5)
    distance = jnp.abs(query_pos[0][:, :, None] - key_pos[0][:, None, :]) + jnp.abs(
        query_pos[1][:, :, None] - key_pos[1][:, None, :]
    )
    scores = scores - slope_vec[None, :, None, None] * distance.astype(jnp.float32)[:, None]
    return jnp.where(key_ocean[:, None, None, :] > 0, scores, -1e30)


def softmax_stats(scores):
    row_max = jnp.max(scores, axis=-1, keepdims=True)
    exps = jnp.exp(scores - row_max)
    return (row_max, jnp.sum(exps, axis=-1, keepdims=True), exps)


def probabilities(query_b, key_b, query_pos, key_pos, key_ocean, slope_vec):
    row_max, row_total, exps = softmax_stats(
        score_table(query_b, key_b, query_pos, key_pos, key_ocean, slope_vec)
    )
    return exps / row_total


def through(probs, query_b, key_b, value_b, masked_b):
    grad_probs = product("bmhe,blhe->bhml", masked_b, value_b)
    grad_value = product("bhml,bmhe->blhe", probs.astype(jnp.bfloat16), masked_b)
    grad_scores = probs * (grad_probs - jnp.sum(probs * grad_probs, axis=-1, keepdims=True))
    scaled = (grad_scores * query_b.shape[-1] ** (-0.5)).astype(jnp.bfloat16)
    grad_query = product("bhml,blhe->bmhe", scaled, key_b)
    grad_key = product("bhml,bmhe->blhe", scaled, query_b)
    return (grad_query, grad_key, grad_value)


def on_device(
    acts_in, first_in, saved_one, cot_one, saved_two, cot_last, gains, slopes, ocean, places
):
    row_count = first_in.shape[0]
    devices = lax.axis_size("seq")
    my_index = lax.axis_index("seq")
    repeats = max(devices // HEADS, 1)
    heads_here = max(HEADS // devices, 1)
    groups = HEADS // heads_here
    channels = heads_here * HD
    my_part = my_index % repeats
    my_group = my_index // repeats
    token_total = devices * row_count
    regions = token_total // REGION
    part_rows = row_count // repeats
    gains_here = lax.dynamic_slice_in_dim(gains[0], my_group * channels, channels, 1).reshape(
        3, heads_here, HD
    )
    slope_here = lax.dynamic_slice_in_dim(slopes[0], my_group * heads_here, heads_here, 0)
    ocean_here = lax.dynamic_slice_in_dim(ocean, my_index * row_count, row_count, 0).astype(
        jnp.float32
    )[:, None]
    key_pos = places.reshape(2, regions, REGION)
    query_pos = lax.dynamic_index_in_dim(
        places.reshape(2, token_total // repeats, repeats), my_part, 2, keepdims=False
    )
    query_pos = query_pos.reshape(2, regions, REGION // repeats)
    key_ocean = ocean.reshape(regions, REGION)

    def by_part(matrix):
        return (
            matrix.reshape(part_rows, repeats, groups, channels)
            .transpose(2, 1, 0, 3)
            .reshape(devices, part_rows, channels)
        )

    def from_parts(received):
        return (
            received.reshape(groups, repeats, part_rows, channels)
            .transpose(2, 1, 0, 3)
            .reshape(row_count, groups * channels)
        )

    def to_heads(normed_in):
        blocks = normed_in.reshape(row_count, groups, channels).transpose(1, 0, 2)
        blocks = jnp.repeat(blocks, repeats, axis=0)
        received = lax.all_to_all(blocks, "seq", split_axis=0, concat_axis=0, tiled=True)
        return received.reshape(token_total, channels)

    def projections(hidden_in):
        hidden_wide = hidden_in.astype(jnp.float32)
        normed_in = normed(hidden_wide).astype(jnp.bfloat16)
        full_heads = to_heads(normed_in)
        query_normed = lax.dynamic_index_in_dim(
            full_heads.reshape(token_total // repeats, repeats, channels),
            my_part,
            1,
            keepdims=False,
        )
        query_normed = query_normed.reshape(regions, REGION // repeats, heads_here, HD)
        key_normed = full_heads.reshape(regions, REGION, heads_here, HD)
        query_b = (query_normed.astype(jnp.float32) * gains_here[0]).astype(jnp.bfloat16)
        key_b = (key_normed.astype(jnp.float32) * gains_here[1]).astype(jnp.bfloat16)
        value_b = (key_normed.astype(jnp.float32) * gains_here[2]).astype(jnp.bfloat16)
        return (hidden_wide, query_normed, key_normed, query_b, key_b, value_b)

    def forward(hidden_in):
        hidden_wide, query_normed, key_normed, query_b, key_b, value_b = projections(hidden_in)
        probs = probabilities(query_b, key_b, query_pos, key_pos, key_ocean, slope_here)
        attended = product("bhml,blhe->bmhe", probs.astype(jnp.bfloat16), value_b).astype(
            jnp.bfloat16
        )
        returned = lax.all_to_all(
            attended.reshape(devices, part_rows, channels),
            "seq",
            split_axis=0,
            concat_axis=0,
            tiled=True,
        )
        return (hidden_wide + ocean_here * from_parts(returned).astype(jnp.float32)).astype(
            jnp.bfloat16
        )

    def backward(hidden_in, cot_in):
        hidden_wide, query_normed, key_normed, query_b, key_b, value_b = projections(hidden_in)
        probs = probabilities(query_b, key_b, query_pos, key_pos, key_ocean, slope_here)
        cot_wide = cot_in.astype(jnp.float32)
        masked_local = (ocean_here * cot_wide).astype(jnp.bfloat16)
        masked_b = lax.all_to_all(
            by_part(masked_local), "seq", split_axis=0, concat_axis=0, tiled=True
        )
        masked_b = masked_b.reshape(regions, REGION // repeats, heads_here, HD)
        grad_query, grad_key, grad_value = through(probs, query_b, key_b, value_b, masked_b)
        key_grads = (grad_key * gains_here[1] + grad_value * gains_here[2]).reshape(
            devices, part_rows, repeats, channels
        )
        query_grads = (grad_query * gains_here[0]).reshape(devices, part_rows, 1, channels)
        slot_mask = (jnp.arange(repeats) == my_part).astype(jnp.float32)[None, None, :, None]
        merged = key_grads + slot_mask * query_grads
        key_wide = key_normed.astype(jnp.float32)
        local_gain = jnp.stack(
            [
                jnp.sum(grad_query * query_normed.astype(jnp.float32), axis=(0, 1)).reshape(
                    channels
                ),
                jnp.sum(grad_key * key_wide, axis=(0, 1)).reshape(channels),
                jnp.sum(grad_value * key_wide, axis=(0, 1)).reshape(channels),
            ]
        )
        gain_part = lax.dynamic_update_slice_in_dim(
            jnp.zeros((3, D), jnp.float32), local_gain, my_group * channels, 1
        )
        received = lax.all_to_all(
            merged.reshape(devices, row_count, channels).astype(jnp.bfloat16),
            "seq",
            split_axis=0,
            concat_axis=0,
            tiled=True,
        ).astype(jnp.float32)
        summed_parts = jnp.sum(received.reshape(groups, repeats, row_count, channels), axis=1)
        grad_normed = summed_parts.transpose(1, 0, 2).reshape(row_count, groups * channels)
        unused, pull_back = jax.vjp(normed, hidden_wide)
        grad_hidden = cot_wide + pull_back(grad_normed)[0]
        return (grad_hidden.astype(jnp.bfloat16), gain_part)

    def summed(gain_part):
        return lax.psum(gain_part, "seq")

    first_out = forward(acts_in[0])
    first_back, first_gain = backward(saved_one[0], cot_one[0])
    from_before = shifted(first_out, "section", 1)
    from_after = shifted(first_back, "section", -1)
    section_index = lax.axis_index("section")
    last_section = lax.axis_size("section") - 1
    second_in = jnp.where(section_index == 0, first_in, from_before)
    second_cot = jnp.where(section_index == last_section, cot_last, from_after)
    gain_first = summed(first_gain)
    second_out = forward(second_in)
    second_back, second_gain = backward(saved_two[0], second_cot)
    gain_total = gain_first + summed(second_gain)
    return (
        first_out[None],
        first_back[None],
        second_out[None],
        second_back[None],
        gain_total[None],
    )


def solution(mesh):
    placed = (
        P("section", "seq", None),
        P("seq", None),
        P("section", "seq", None),
        P("section", "seq", None),
        P("section", "seq", None),
        P("seq", None),
        P("section", None, None),
        P("section", None),
        P(),
        P(),
    )
    return jax.shard_map(
        on_device,
        mesh=mesh,
        in_specs=placed,
        out_specs=(
            P("section", "seq", None),
            P("section", "seq", None),
            P("section", "seq", None),
            P("section", "seq", None),
            P("section", None, None),
        ),
        check_vma=False,
    )
```

profile of v0, /device:TPU:32, one launch (start us, length us, event | category | flops | bytes accessed | tf_op | source)
XLA Modules:
  0.0 1047.3 jit_solution(12042072658765216958)
XLA Ops:
  4.6 13.7 %all-to-all-start.3 = ((bf16[64,64,128]{2,1,0:T(8,128)(2,1)}), bf16[64,64,128]{2,1,0:T(8,128)(2,1)S(1)}, u32[]{:S(2)}, u32[]{:S(2)}) async-start(bf16[64,64,128]{2,1,0:T(8,128)(2,1)} %bitcast.24), calls=%async_computation.3 | async-start | bytes 2097152 | tf_op jit(solution)/shard_map/all_to_all | solution.py:148
  19.9 29.7 %all-to-all-done.3 = bf16[64,64,128]{2,1,0:T(8,128)(2,1)S(1)} async-done(((bf16[64,64,128]{2,1,0:T(8,128)(2,1)}), bf16[64,64,128]{2,1,0:T(8,128)(2,1)S(1)}, u32[]{:S(2)}, u32[]{:S(2)}) %all-to-all-start.3) | async-done | bytes 1048608 | tf_op jit(solution)/shard_map/all_to_all | solution.py:148
  64.3 45.4 %all-to-all-done = bf16[64,128,128]{2,1,0:T(8,128)(2,1)} async-done(((bf16[64,128,128]{2,1,0:T(8,128)(2,1)}), bf16[64,128,128]{2,1,0:T(8,128)(2,1)}, u32[]{:S(2)}, u32[]{:S(2)}) %all-to-all-start) | async-done | bytes 2097184 | tf_op jit(solution)/shard_map/all_to_all | solution.py:106
  119.1 6.4 reshape.606
  135.4 6.4 subtract_select_fusion.3
  144.8 12.3 %fusion.78 = bf16[32,128,128]{1,2,0:T(8,128)(2,1)} fusion(bf16[32,256,128]{2,1,0:T(8,128)(2,1)} %bitcast.8, f32[128]{0:T(128)S(1)} %get-tuple-element.62, f32[32,128]{1,0:T(8,128)S(1)} %fusion.107, f32[32,128,256]{2,1,0:T(8,128)} %copy-done.30), kind=kOutput, calls=%fused_computation.141 | convolution fusion | flops 275255552 | bytes 7356928 | tf_op jit(solution)/shard_map/bhml,blhe->bmhe/dot_general | solution.py:25
  157.2 9.8 all-to-all-done.2
  182.0 16.9 %all-to-all-done.1 = bf16[64,64,128]{2,1,0:T(8,128)(2,1)} async-done(((bf16[64,64,128]{2,1,0:T(8,128)(2,1)}), bf16[64,64,128]{2,1,0:T(8,128)(2,1)}, u32[]{:S(2)}, u32[]{:S(2)}) %all-to-all-start.1) | async-done | bytes 1048608 | tf_op jit(solution)/shard_map/all_to_all | solution.py:132
  216.1 29.8 %collective-permute-done = bf16[128,4096]{1,0:T(8,128)(2,1)} collective-permute-done((bf16[128,4096]{1,0:T(8,128)(2,1)}, bf16[128,4096]{1,0:T(8,128)(2,1)}, u32[]{:S(2)}, u32[]{:S(2)}) %collective-permute-start) | collective-permute-done | bytes 1048608 | tf_op jit(solution)/shard_map/ppermute | solution.py:15
  256.4 10.5 %all-to-all-start.5 = ((bf16[64,128,128]{2,1,0:T(8,128)(2,1)}), bf16[64,128,128]{2,1,0:T(8,128)(2,1)}, u32[]{:S(2)}, u32[]{:S(2)}) async-start(bf16[64,128,128]{2,1,0:T(8,128)(2,1)} %bitcast.289), calls=%async_computation.5 | async-start | bytes 4194304 | tf_op jit(solution)/shard_map/all_to_all | solution.py:106
  293.0 23.3 %all-to-all-done.5 = bf16[64,128,128]{2,1,0:T(8,128)(2,1)} async-done(((bf16[64,128,128]{2,1,0:T(8,128)(2,1)}), bf16[64,128,128]{2,1,0:T(8,128)(2,1)}, u32[]{:S(2)}, u32[]{:S(2)}) %all-to-all-start.5) | async-done | bytes 2097184 | tf_op jit(solution)/shard_map/all_to_all | solution.py:106
  329.9 13.1 %fusion.68 = f32[32,128,256]{2,1,0:T(8,128)} fusion(bf16[32,128,128]{2,1,0:T(8,128)(2,1)S(1)} %bitcast.295, f32[32,128]{1,0:T(8,128)S(1)} %get-tuple-element.70, f32[32,128,256]{2,1,0:T(8,128)} %copy-done.31), kind=kOutput, calls=%fused_computation.126 | convolution fusion | flops 271585536 | bytes 9453568 | tf_op jit(solution)/shard_map/bhml,bmhe->blhe/dot_general | solution.py:25
  343.0 31.3 %fusion.15 = (f32[128]{0:T(128)S(1)}, f32[128]{0:T(128)S(1)}, f32[32,256,1,128]{1,3,0,2:T(8,128)}) fusion(f32[32,256,1,128]{1,3,0,2:T(8,128)} %copy.169, f32[32,128,256]{2,1,0:T(8,128)} %fusion.68, f32[128]{0:T(128)S(1)} %get-tuple-element.62, f32[128]{0:T(128)S(1)} %get-tuple-element.60, bf16[32,128,128]{2,1,0:T(8,128)(2,1)S(1)} %copy-done.37, ...), kind=kOutput, calls=%fused_computation.29 | convolution fusion | flops 283119616 | bytes 22038528 | tf_op jit(solution)/shard_map/bhml,bmhe->blhe/dot_general | solution.py:25
  380.0 27.6 %fusion.59 = (f32[128]{0:T(128)S(1)}, f32[32,128,1,128]{3,1,0,2:T(8,128)}) fusion(f32[32,128,1,128]{3,1,0,2:T(8,128)S(1)} %bitcast.285, f32[128]{0:T(128)S(1)} %get-tuple-element.61, bf16[32,256,128]{2,1,0:T(8,128)(2,1)} %get-tuple-element.55, f32[32,128,256]{2,1,0:T(8,128)} %fusion.119, f32[32,128,256]{2,1,0:T(8,128)} %get-tuple-element.71, ...), kind=kOutput, calls=%fused_computation.102 | convolution fusion | flops 277352576 | bytes 14697472 | tf_op jit(solution)/shard_map/bhml,blhe->bmhe/dot_general | solution.py:25
  429.4 12.3 %fusion.81 = bf16[32,128,128]{1,2,0:T(8,128)(2,1)} fusion(bf16[32,256,128]{2,1,0:T(8,128)(2,1)} %bitcast.44, f32[128]{0:T(128)S(1)} %get-tuple-element.62, f32[32,128]{1,0:T(8,128)S(1)} %fusion.113, f32[32,128,256]{2,1,0:T(8,128)} %copy-done.32), kind=kOutput, calls=%fused_computation.142 | convolution fusion | flops 275255552 | bytes 7356928 | tf_op jit(solution)/shard_map/bhml,blhe->bmhe/dot_general | solution.py:25
  441.8 26.1 %all-to-all-done.4 = bf16[64,128,128]{2,1,0:T(8,128)(2,1)} async-done(((bf16[64,128,128]{2,1,0:T(8,128)(2,1)}), bf16[64,128,128]{2,1,0:T(8,128)(2,1)}, u32[]{:S(2)}, u32[]{:S(2)}) %all-to-all-start.4) | async-done | bytes 2097184 | tf_op jit(solution)/shard_map/all_to_all | solution.py:172
  467.8 7.8 all-to-all-start.6
  489.0 11.8 %all-to-all-done.6 = bf16[64,64,128]{2,1,0:T(8,128)(2,1)} async-done(((bf16[64,64,128]{2,1,0:T(8,128)(2,1)}), bf16[64,64,128]{2,1,0:T(8,128)(2,1)}, u32[]{:S(2)}, u32[]{:S(2)}) %all-to-all-start.6) | async-done | bytes 1048608 | tf_op jit(solution)/shard_map/all_to_all | solution.py:132
  509.6 14.1 %all-to-all-start.8 = ((bf16[64,64,128]{2,1,0:T(8,128)(2,1)}), bf16[64,64,128]{2,1,0:T(8,128)(2,1)S(1)}, u32[]{:S(2)}, u32[]{:S(2)}) async-start(bf16[64,64,128]{2,1,0:T(8,128)(2,1)} %bitcast.61), calls=%async_computation.8 | async-start | bytes 2097152 | tf_op jit(solution)/shard_map/all_to_all | solution.py:148
  545.5 13.5 %fusion.66 = f32[32,128,256]{2,1,0:T(8,128)} fusion(bf16[32,128,128]{2,1,0:T(8,128)(2,1)} %bitcast.296, f32[32,128]{1,0:T(8,128)S(1)} %get-tuple-element.72, f32[32,128,256]{2,1,0:T(8,128)} %copy-done.29), kind=kOutput, calls=%fused_computation.119 | convolution fusion | flops 271585536 | bytes 9453568 | tf_op jit(solution)/shard_map/bhml,bmhe->blhe/dot_general | solution.py:25
  562.9 32.3 %fusion.12 = (f32[128]{0:T(128)S(1)}, f32[128]{0:T(128)S(1)}, f32[32,256,1,128]{1,3,0,2:T(8,128)}) fusion(f32[32,256,1,128]{1,3,0,2:T(8,128)} %copy.171, f32[32,128,256]{2,1,0:T(8,128)} %fusion.66, f32[128]{0:T(128)S(1)} %get-tuple-element.62, f32[128]{0:T(128)S(1)} %get-tuple-element.60, bf16[32,128,128]{2,1,0:T(8,128)(2,1)} %get-tuple-element.65, ...), kind=kOutput, calls=%fused_computation.22 | convolution fusion | flops 283119616 | bytes 22038528 | tf_op jit(solution)/shard_map/bhml,bmhe->blhe/dot_general | solution.py:25
  601.0 27.8 %fusion.58 = (f32[128]{0:T(128)S(1)}, f32[32,128,1,128]{3,1,0,2:T(8,128)}) fusion(f32[32,128,1,128]{3,1,0,2:T(8,128)S(1)} %bitcast.283, f32[128]{0:T(128)S(1)} %get-tuple-element.61, bf16[32,256,128]{2,1,0:T(8,128)(2,1)} %get-tuple-element.63, f32[32,128,256]{2,1,0:T(8,128)} %fusion.120, f32[32,128,256]{2,1,0:T(8,128)} %get-tuple-element.73, ...), kind=kOutput, calls=%fused_computation.99 | convolution fusion | flops 277352576 | bytes 14697472 | tf_op jit(solution)/shard_map/bhml,blhe->bmhe/dot_general | solution.py:25
  634.5 7.4 all-to-all-start.9
  655.0 378.8 %psum.16 = f32[3,4096]{1,0:T(4,128)S(1)} all-reduce(f32[3,4096]{1,0:T(4,128)S(1)} %constant_dynamic-update-slice_fusion), channel_id=1, replica_groups=mesh['section'=4,'seq'=64] {'seq'}, use_global_device_ids=true, to_apply=%region_21.22 | all-reduce | flops 12288 | bytes 98304 | tf_op jit(solution)/shard_map/psum | solution.py:186
  (189 shorter events, 237.7 us)
Async XLA Ops:
  0.6 125.1 %copy-start = (f32[1,32]{1,0:T(1,128)S(1)}, f32[1,32]{1,0:T(1,128)}, u32[]{:S(2)}) copy-start(f32[1,32]{1,0:T(1,128)} %param.17) | copy-start | bytes 388
  2.5 15.8 %copy-start.11 = (bf16[1,128,4096]{2,1,0:T(8,128)(2,1)S(1)}, bf16[1,128,4096]{2,1,0:T(8,128)(2,1)}, u32[]{:S(2)}) copy-start(bf16[1,128,4096]{2,1,0:T(8,128)(2,1)} %param.10) | copy-start | bytes 3145732
  4.6 44.9 %all-to-all-start.3 = ((bf16[64,64,128]{2,1,0:T(8,128)(2,1)}), bf16[64,64,128]{2,1,0:T(8,128)(2,1)S(1)}, u32[]{:S(2)}, u32[]{:S(2)}) async-start(bf16[64,64,128]{2,1,0:T(8,128)(2,1)} %bitcast.24), calls=%async_computation.3 | async-start | bytes 2097152 | tf_op jit(solution)/shard_map/all_to_all | solution.py:148
  51.4 58.3 %all-to-all-start = ((bf16[64,128,128]{2,1,0:T(8,128)(2,1)}), bf16[64,128,128]{2,1,0:T(8,128)(2,1)}, u32[]{:S(2)}, u32[]{:S(2)}) async-start(bf16[64,128,128]{2,1,0:T(8,128)(2,1)} %bitcast.2), calls=%async_computation | async-start | bytes 4194304 | tf_op jit(solution)/shard_map/all_to_all | solution.py:106
  58.4 54.5 %copy-start.4 = (f32[1,128,4096]{1,2,0:T(8,128)}, f32[1,128,4096]{1,2,0:T(8,128)S(1)}, u32[]{:S(2)}) copy-start(f32[1,128,4096]{1,2,0:T(8,128)S(1)} %copy.146) | copy-start | bytes 6291460
  64.3 54.9 %copy-start.38 = (s32[2,8192]{1,0:T(2,128)S(1)}, s32[2,8192]{1,0:T(2,128)}, u32[]{:S(2)}) copy-start(s32[2,8192]{1,0:T(2,128)} %param.19) | copy-start | bytes 196612
  113.0 54.1 %all-to-all-start.2 = ((bf16[64,128,128]{2,1,0:T(8,128)(2,1)}), bf16[64,128,128]{2,1,0:T(8,128)(2,1)S(1)}, u32[]{:S(2)}, u32[]{:S(2)}) async-start(bf16[64,128,128]{2,1,0:T(8,128)(2,1)} %bitcast.287), calls=%async_computation.2 | async-start | bytes 4194304 | tf_op jit(solution)/shard_map/all_to_all | solution.py:106
  167.0 31.9 %all-to-all-start.1 = ((bf16[64,64,128]{2,1,0:T(8,128)(2,1)}), bf16[64,64,128]{2,1,0:T(8,128)(2,1)}, u32[]{:S(2)}, u32[]{:S(2)}) async-start(bf16[64,64,128]{2,1,0:T(8,128)(2,1)} %bitcast.304), calls=%async_computation.1 | async-start | bytes 2097152 | tf_op jit(solution)/shard_map/all_to_all | solution.py:132
  202.2 50.9 %all-to-all-start.7 = ((bf16[64,128,128]{2,1,0:T(8,128)(2,1)}), bf16[64,128,128]{2,1,0:T(8,128)(2,1)}, u32[]{:S(2)}, u32[]{:S(2)}) async-start(bf16[64,128,128]{2,1,0:T(8,128)(2,1)} %bitcast.288), calls=%async_computation.7 | async-start | bytes 4194304 | tf_op jit(solution)/shard_map/all_to_all | solution.py:106
  214.2 31.7 %collective-permute-start = (bf16[128,4096]{1,0:T(8,128)(2,1)}, bf16[128,4096]{1,0:T(8,128)(2,1)}, u32[]{:S(2)}, u32[]{:S(2)}) collective-permute-start(bf16[128,4096]{1,0:T(8,128)(2,1)} %fusion.43), channel_id=1, source_target_pairs={{0,64},{64,128},{128,192},{1,65},{65,129},{129,193},{2,66},{66,130... | collective-permute-start | bytes 3145736 | tf_op jit(solution)/shard_map/ppermute | solution.py:15
  256.4 60.0 %all-to-all-start.5 = ((bf16[64,128,128]{2,1,0:T(8,128)(2,1)}), bf16[64,128,128]{2,1,0:T(8,128)(2,1)}, u32[]{:S(2)}, u32[]{:S(2)}) async-start(bf16[64,128,128]{2,1,0:T(8,128)(2,1)} %bitcast.289), calls=%async_computation.5 | async-start | bytes 4194304 | tf_op jit(solution)/shard_map/all_to_all | solution.py:106
  277.3 9.2 copy-start.2
  277.3 9.2 copy-start.3
  290.4 29.7 %copy-start.19 = (f32[4096,1,128]{2,1,0:T(1,128)S(1)}, f32[4096,1,128]{2,1,0:T(1,128)}, u32[]{:S(2)}) copy-start(f32[4096,1,128]{2,1,0:T(1,128)} %dynamic-slice_convert_fusion) | copy-start | bytes 6291460
  329.9 13.1 %copy-start.37 = (bf16[32,128,128]{2,1,0:T(8,128)(2,1)S(1)}, bf16[32,128,128]{2,1,0:T(8,128)(2,1)}, u32[]{:S(2)}) copy-start(bf16[32,128,128]{2,1,0:T(8,128)(2,1)} %copy-done.36) | copy-start | bytes 3145732
  413.2 54.7 %all-to-all-start.4 = ((bf16[64,128,128]{2,1,0:T(8,128)(2,1)}), bf16[64,128,128]{2,1,0:T(8,128)(2,1)}, u32[]{:S(2)}, u32[]{:S(2)}) async-start(bf16[64,128,128]{2,1,0:T(8,128)(2,1)} %add_convert_fusion.1), calls=%async_computation.4 | async-start | bytes 4194304 | tf_op jit(solution)/shard_map/all_to_all | solution.py:172
  441.8 36.2 %copy-start.23 = (f32[128,32,128]{2,0,1:T(8,128)S(1)}, f32[128,32,128]{2,0,1:T(8,128)}, u32[]{:S(2)}) copy-start(f32[128,32,128]{2,0,1:T(8,128)} %copy.154) | copy-start | bytes 6291460
  467.8 32.9 %all-to-all-start.6 = ((bf16[64,64,128]{2,1,0:T(8,128)(2,1)}), bf16[64,64,128]{2,1,0:T(8,128)(2,1)}, u32[]{:S(2)}, u32[]{:S(2)}) async-start(bf16[64,64,128]{2,1,0:T(8,128)(2,1)} %bitcast.303), calls=%async_computation.6 | async-start | bytes 2097152 | tf_op jit(solution)/shard_map/all_to_all | solution.py:132
  487.0 16.5 %collective-permute-start.1 = (bf16[128,4096]{1,0:T(8,128)(2,1)}, bf16[128,4096]{1,0:T(8,128)(2,1)}, u32[]{:S(2)}, u32[]{:S(2)}) collective-permute-start(bf16[128,4096]{1,0:T(8,128)(2,1)} %fusion.47), channel_id=1, source_target_pairs={{64,0},{128,64},{192,128},{65,1},{129,65},{193,129},{66,2},{130,66... | collective-permute-start | bytes 3145736 | tf_op jit(solution)/shard_map/ppermute | solution.py:15
  488.9 14.6 %copy-start.17 = (bf16[128,4096]{1,0:T(8,128)(2,1)S(1)}, bf16[128,4096]{1,0:T(8,128)(2,1)}, u32[]{:S(2)}) copy-start(bf16[128,4096]{1,0:T(8,128)(2,1)} %copy-done.16) | copy-start | bytes 3145732
  509.6 34.9 %all-to-all-start.8 = ((bf16[64,64,128]{2,1,0:T(8,128)(2,1)}), bf16[64,64,128]{2,1,0:T(8,128)(2,1)S(1)}, u32[]{:S(2)}, u32[]{:S(2)}) async-start(bf16[64,64,128]{2,1,0:T(8,128)(2,1)} %bitcast.61), calls=%async_computation.8 | async-start | bytes 2097152 | tf_op jit(solution)/shard_map/all_to_all | solution.py:148
  545.5 13.5 %copy-start.18 = (bf16[32,256,128]{2,1,0:T(8,128)(2,1)S(1)}, bf16[32,256,128]{2,1,0:T(8,128)(2,1)}, u32[]{:S(2)}) copy-start(bf16[32,256,128]{2,1,0:T(8,128)(2,1)} %get-tuple-element.64) | copy-start | bytes 6291460
  634.5 7.4 copy-start.6
  634.5 399.9 %all-to-all-start.9 = ((bf16[64,128,128]{2,1,0:T(8,128)(2,1)}), bf16[64,128,128]{2,1,0:T(8,128)(2,1)}, u32[]{:S(2)}, u32[]{:S(2)}) async-start(bf16[64,128,128]{2,1,0:T(8,128)(2,1)} %add_convert_fusion), calls=%async_computation.9 | async-start | bytes 4194304 | tf_op jit(solution)/shard_map/all_to_all | solution.py:172
  (28 other events, 93.6 us)
where the time goes:
time: 1060 us; the launch traced here: 1050 us
  blocking collectives  379 us (36%)
  waiting for transfers between devices  201 us (19%)
  matrix products  197 us (19%)
  local copies, waits for them, and re-layouts  99.9 us (9%)
  starting transfers between devices  86.4 us (8%)
  other arithmetic  81.9 us (8%)
    psum x1, blocking collectives, summed(): return lax.psum(gain_part, 'seq')  379 us
    dot_general x14, matrix products, product(): jnp.einsum(einsum_form, left, right, preferred_element_type=jnp.float32)  197 us
    all_to_all x4, waiting for transfers between devices, to_heads(): lax.all_to_all(blocks, 'seq', split_axis=0, concat_axis=0, tiled=True)  81 us
    all_to_all x2, waiting for transfers between devices, backward(): lax.all_to_all(by_part(masked_local), 'seq', split_axis=0, concat_axis=0,...  35.5 us
    ppermute x2, waiting for transfers between devices, shifted(): lax.ppermute(value, axis, [(source, source + steps) for source in range(i...  29.8 us
    all_to_all x2, waiting for transfers between devices, forward(): lax.all_to_all(attended.reshape(devices, part_rows, channels), 'seq', spl...  28.7 us
    all_to_all x4, starting transfers between devices, to_heads(): lax.all_to_all(blocks, 'seq', split_axis=0, concat_axis=0, tiled=True)  27.8 us
    all_to_all x2, starting transfers between devices, backward(): lax.all_to_all(by_part(masked_local), 'seq', split_axis=0, concat_axis=0,...  27.8 us
  transfers between devices with their start and end apart: 12, of which 10 were waited for; matrix products, arithmetic and copies ran while one was open for 14% of the time, Pallas kernels for 0%

commit v1 on v0

v1 whole, which is shorter than its diff:
```python
import functools

import jax
import jax.numpy as jnp
from jax import lax
from jax.experimental import pallas as pl
from jax.experimental.pallas import tpu as pltpu
from jax.sharding import PartitionSpec as P

D = 4096
HEADS = 32
HD = 128
REGION = 256
OWN = 128
HALF = D // 2
LOG2E = 1.4426950408889634
SCALE = HD ** (-0.5)
FAR = 1e30
STEP_HEADS = 4
VMEM_LIMIT = 48 * 1024 * 1024


def dot(left, right, left_dim, right_dim):
    return lax.dot_general(
        left,
        right,
        (((left_dim,), (right_dim,)), ((), ())),
        preferred_element_type=jnp.float32,
    )


def rows_of(own_ref, other_ref, cols):
    return jnp.concatenate([own_ref[:, cols], other_ref[:, cols]], axis=0).astype(jnp.float32)


def forward_body(
    query_rows, heads, own_ref, other_ref, inverse_ref, gains_ref, slopes_ref, table_ref, keep_ref, *out_refs
):
    step = pl.program_id(0)
    inverse = inverse_ref[...]
    keep = keep_ref[:query_rows]
    ones = jnp.ones((REGION, HD), jnp.bfloat16)
    for head in range(heads):
        cols = pl.ds(head * HD, HD)
        gains = gains_ref[:, cols]
        hidden = rows_of(own_ref, other_ref, cols)
        normed_in = (hidden * inverse).astype(jnp.bfloat16).astype(jnp.float32)
        query = (normed_in[:query_rows] * gains[0:1]).astype(jnp.bfloat16)
        key = (normed_in * gains[1:2]).astype(jnp.bfloat16)
        value = (normed_in * gains[2:3]).astype(jnp.bfloat16)
        slope = slopes_ref[0, step * heads + head] * LOG2E
        scores = dot(query, key, 1, 1) * (SCALE * LOG2E) - slope * table_ref[:query_rows]
        exps = jnp.exp2(scores - jnp.max(scores, axis=1, keepdims=True)).astype(jnp.bfloat16)
        mixed = dot(exps, jnp.concatenate([value, ones], axis=1), 1, 0)
        attended = (mixed[:, :HD] / mixed[:, HD:]).astype(jnp.bfloat16).astype(jnp.float32)
        result = (hidden[:query_rows] + keep * attended).astype(jnp.bfloat16)
        out_refs[0][:, cols] = result[:OWN]
        if query_rows == REGION:
            out_refs[1][:, cols] = result[OWN:]


def forward(query_rows, own, other, inverse, gains, slopes, table, keep):
    width = STEP_HEADS * HD
    wide = pl.BlockSpec((OWN, width), lambda j: (0, j))
    whole = lambda shape: pl.BlockSpec(shape, lambda j: (0, 0))
    outs = query_rows // OWN
    return pl.pallas_call(
        functools.partial(forward_body, query_rows, STEP_HEADS),
        grid=(D // width,),
        in_specs=[
            wide,
            wide,
            whole((REGION, 1)),
            pl.BlockSpec((3, width), lambda j: (0, j)),
            pl.BlockSpec(memory_space=pltpu.SMEM),
            whole((REGION, REGION)),
            whole((REGION, 1)),
        ],
        out_specs=[wide] * outs,
        out_shape=[jax.ShapeDtypeStruct((OWN, D), jnp.bfloat16)] * outs,
        compiler_params=pltpu.CompilerParams(vmem_limit_bytes=VMEM_LIMIT),
        cost_estimate=pl.CostEstimate(
            flops=4 * query_rows * REGION * D,
            bytes_accessed=4 * OWN * D * (1 + outs),
            transcendentals=query_rows * REGION * HEADS,
        ),
        name="attend" + str(query_rows),
    )(own, other, inverse, gains, slopes, table, keep)


def backward_body(
    heads,
    side_ref,
    own_ref,
    other_ref,
    cot_own_ref,
    cot_other_ref,
    inverse_ref,
    gains_ref,
    slopes_ref,
    table_ref,
    keep_ref,
    grad_ref,
    gain_ref,
    moment_ref,
    total_ref,
):
    step = pl.program_id(0)
    first_head = side_ref[0] * (HEADS // 2) + step * heads
    inverse = inverse_ref[...]
    keep = keep_ref[...]

    @pl.when(step == 0)
    def _():
        total_ref[...] = jnp.zeros_like(total_ref)

    for head in range(heads):
        cols = pl.ds(head * HD, HD)
        gains = gains_ref[:, cols]
        wide = rows_of(own_ref, other_ref, cols) * inverse
        normed_in = wide.astype(jnp.bfloat16).astype(jnp.float32)
        query = (normed_in * gains[0:1]).astype(jnp.bfloat16)
        key = (normed_in * gains[1:2]).astype(jnp.bfloat16)
        value = (normed_in * gains[2:3]).astype(jnp.bfloat16)
        masked = (rows_of(cot_own_ref, cot_other_ref, cols) * keep).astype(jnp.bfloat16)
        slope = slopes_ref[0, first_head + head] * LOG2E
        scores = dot(key, query, 1, 1) * (SCALE * LOG2E) - slope * table_ref[...]
        exps = jnp.exp2(scores - jnp.max(scores, axis=0, keepdims=True))
        probs = exps * (1.0 / jnp.sum(exps, axis=0, keepdims=True))
        grad_probs = dot(value, masked, 1, 1)
        inner = jnp.sum(probs * grad_probs, axis=0, keepdims=True)
        grad_scores = (probs * (grad_probs - inner) * SCALE).astype(jnp.bfloat16)
        grad_value = dot(probs.astype(jnp.bfloat16), masked, 1, 0)
        grad_key = dot(grad_scores, query, 1, 0)
        grad_query = dot(grad_scores, key, 0, 0)
        grad = grad_query * gains[0:1] + grad_key * gains[1:2] + grad_value * gains[2:3]
        grad_ref[:, cols] = grad
        total_ref[...] += grad * wide
        gain_ref[0:1, cols] = jnp.sum(grad_query * normed_in, axis=0, keepdims=True)
        gain_ref[1:2, cols] = jnp.sum(grad_key * normed_in, axis=0, keepdims=True)
        gain_ref[2:3, cols] = jnp.sum(grad_value * normed_in, axis=0, keepdims=True)

    @pl.when(step == pl.num_programs(0) - 1)
    def _():
        moment_ref[...] = jnp.sum(total_ref[...], axis=1, keepdims=True)


def backward(side, own, other, cot_own, cot_other, inverse, gains, slopes, table, keep):
    width = STEP_HEADS * HD
    steps = HALF // width
    half = pl.BlockSpec((OWN, width), lambda j, s: (0, j))

    def block(array):
        if array.shape[1] == HALF:
            return half
        return pl.BlockSpec((array.shape[0], width), lambda j, s: (0, s[0] * steps + j))

    whole = lambda shape: pl.BlockSpec(shape, lambda j, s: (0, 0))
    return pl.pallas_call(
        functools.partial(backward_body, STEP_HEADS),
        grid_spec=pltpu.PrefetchScalarGridSpec(
            num_scalar_prefetch=1,
            grid=(steps,),
            in_specs=[
                block(own),
                block(other),
                block(cot_own),
                block(cot_other),
                whole((REGION, 1)),
                block(gains),
                pl.BlockSpec(memory_space=pltpu.SMEM),
                whole((REGION, REGION)),
                whole((REGION, 1)),
            ],
            out_specs=[
                pl.BlockSpec((REGION, width), lambda j, s: (0, j)),
                pl.BlockSpec((3, width), lambda j, s: (0, j)),
                whole((REGION, 1)),
            ],
            scratch_shapes=[pltpu.VMEM((REGION, HD), jnp.float32)],
        ),
        out_shape=[
            jax.ShapeDtypeStruct((REGION, HALF), jnp.float32),
            jax.ShapeDtypeStruct((3, HALF), jnp.float32),
            jax.ShapeDtypeStruct((REGION, 1), jnp.float32),
        ],
        compiler_params=pltpu.CompilerParams(vmem_limit_bytes=VMEM_LIMIT),
        cost_estimate=pl.CostEstimate(
            flops=10 * REGION * REGION * HALF,
            bytes_accessed=4 * REGION * HALF + 4 * REGION * HALF,
            transcendentals=REGION * REGION * HEADS // 2,
        ),
        name="differentiate",
    )(side, own, other, cot_own, cot_other, inverse, gains, slopes, table, keep)


def combine_body(
    side_ref, own_ref, other_ref, cot_own_ref, cot_other_ref, grad_ref, inverse_ref, moment_ref, out_own, out_other
):
    inverse = inverse_ref[...]
    mean = moment_ref[...] * (1.0 / D)
    for rows, hidden, cot, out in (
        (slice(0, OWN), own_ref, cot_own_ref, out_own),
        (slice(OWN, REGION), other_ref, cot_other_ref, out_other),
    ):
        scale = inverse[rows]
        wide = hidden[...].astype(jnp.float32) * scale
        grad = (grad_ref[rows] - wide * mean[rows]) * scale
        out[...] = (cot[...].astype(jnp.float32) + grad).astype(jnp.bfloat16)


def combine(side, own, other, cot_own, cot_other, grad, inverse, moment):
    width = STEP_HEADS * HD
    steps = HALF // width
    half = pl.BlockSpec((OWN, width), lambda j, s: (0, j))

    def block(array):
        if array.shape[1] == HALF:
            return half
        return pl.BlockSpec((array.shape[0], width), lambda j, s: (0, s[0] * steps + j))

    whole = pl.BlockSpec((REGION, 1), lambda j, s: (0, 0))
    return pl.pallas_call(
        combine_body,
        grid_spec=pltpu.PrefetchScalarGridSpec(
            num_scalar_prefetch=1,
            grid=(steps,),
            in_specs=[
                block(own),
                block(other),
                block(cot_own),
                block(cot_other),
                pl.BlockSpec((REGION, width), lambda j, s: (0, j)),
                whole,
                whole,
            ],
            out_specs=[half, half],
        ),
        out_shape=[jax.ShapeDtypeStruct((OWN, HALF), jnp.bfloat16)] * 2,
        compiler_params=pltpu.CompilerParams(vmem_limit_bytes=VMEM_LIMIT),
        cost_estimate=pl.CostEstimate(
            flops=6 * REGION * HALF, bytes_accessed=10 * REGION * HALF, transcendentals=0
        ),
        name="combine",
    )(side, own, other, cot_own, cot_other, grad, inverse, moment)


def after(value, *earlier):
    return lax.optimization_barrier((value, earlier))[0]


def inverse_norm(hidden):
    wide = hidden.astype(jnp.float32)
    return lax.rsqrt(jnp.mean(wide * wide, axis=1, keepdims=True) + 1e-05)


def on_device(
    acts_in, first_in, saved_one, cot_one, saved_two, cot_last, gains, slopes, ocean, places
):
    devices = lax.axis_size("seq")
    sections = lax.axis_size("section")
    my_index = lax.axis_index("seq")
    section_index = lax.axis_index("section")
    side = my_index % 2
    side_vec = side.astype(jnp.int32)[None]
    acts, saved_a, cot_a, saved_b = (acts_in[0], saved_one[0], cot_one[0], saved_two[0])
    gain_rows = gains[0]
    partners = [(i, i ^ 1) for i in range(devices)]

    def swap(value):
        return lax.ppermute(value, "seq", partners)

    def swap_in(section, value):
        base = section * devices
        return lax.ppermute(
            value, ("section", "seq"), [(base + i, base + (i ^ 1)) for i in range(devices)]
        )

    def shifted(value, steps):
        first, last = (max(0, -steps), min(sections, sections - steps))
        return lax.ppermute(value, "section", [(s, s + steps) for s in range(first, last)])

    def for_partner(matrix):
        return lax.dynamic_slice_in_dim(matrix, (1 - side) * HALF, HALF, 1)

    def for_me(matrix):
        return lax.dynamic_slice_in_dim(matrix, side * HALF, HALF, 1)

    def joined(mine, received):
        pair = jnp.concatenate([mine, received], axis=1)
        flipped = jnp.concatenate([received, mine], axis=1)
        return jnp.where(side == 0, pair, flipped)

    def whole_rows(moment):
        received = swap(moment)
        return moment + jnp.concatenate([received[OWN:], received[:OWN]], axis=0)

    def region_order(vector):
        own = lax.dynamic_slice_in_dim(vector, my_index * OWN, OWN, vector.ndim - 1)
        start = (my_index + 1 - 2 * side) * OWN
        other = lax.dynamic_slice_in_dim(vector, start, OWN, vector.ndim - 1)
        return jnp.concatenate([own, other], axis=-1)

    place = region_order(places)
    wet = region_order(ocean)
    distance = (
        jnp.abs(place[0][:, None] - place[0][None, :])
        + jnp.abs(place[1][:, None] - place[1][None, :])
    ).astype(jnp.float32)
    by_query = jnp.where(wet[None, :] > 0, distance, FAR)
    by_key = jnp.where(wet[:, None] > 0, distance, FAR)
    keep = wet.astype(jnp.float32)[:, None]

    saved_a_other = swap(for_partner(saved_a))
    cot_a_other = swap(for_partner(cot_a))
    own_inverse = jnp.concatenate([inverse_norm(saved_a), inverse_norm(saved_b)], axis=1)
    other_inverse = swap(own_inverse)
    inverse_ab = jnp.concatenate([own_inverse, other_inverse], axis=0)
    inverse_a, inverse_b = (inverse_ab[:, 0:1], inverse_ab[:, 1:2])

    saved_b_send = after(for_partner(saved_b), saved_a_other)
    saved_b_other = swap(saved_b_send)
    cot_last_other = swap_in(sections - 1, after(for_partner(cot_last), saved_a_other))
    acts_other = swap(after(acts, saved_b_other))

    back = (side_vec, saved_a, saved_a_other, cot_a, cot_a_other)
    grad, gain_a, moment = backward(*back, inverse_a, gain_rows, slopes, by_key, keep)
    moment = whole_rows(moment)
    first_own, first_other = combine(*back, grad, inverse_a, moment)
    grad_one_part = swap(after(first_other, acts_other))
    next_own, next_other = (shifted(first_own, -1), shifted(first_other, -1))

    is_last = section_index == sections - 1
    cot_b_own = jnp.where(is_last, for_me(cot_last), next_own)
    cot_b_other = jnp.where(is_last, cot_last_other, next_other)
    back = (side_vec, saved_b, saved_b_other, cot_b_own, cot_b_other)
    grad, gain_b, moment = backward(*back, inverse_b, gain_rows, slopes, by_key, keep)
    moment = whole_rows(moment)
    second_own, second_other = combine(*back, grad, inverse_b, moment)
    bwd_two_part = swap(after(second_other, acts_other))

    first_in_other = swap_in(0, after(first_in, acts_other))

    gain = gain_a + gain_b
    bit = 2
    while bit < devices:
        terms = [gain]
        for flip in ([bit] if bit == 2 else [bit, 2 * bit, 3 * bit]):
            terms.append(lax.ppermute(gain, "seq", [(i, i ^ flip) for i in range(devices)]))
        if bit == 2:
            gain = terms[0] + terms[1]
            bit = 4
        else:
            gain = (terms[0] + terms[1]) + (terms[2] + terms[3])
            bit = 4 * bit
    gain_total = joined(gain, swap(gain))

    inverse = jnp.concatenate([inverse_norm(acts), inverse_norm(acts_other)], axis=0)
    out_own, out_other = forward(
        REGION, acts, acts_other, inverse, gain_rows, slopes, by_query, keep
    )
    is_first = section_index == 0
    in_own = jnp.where(is_first, first_in, shifted(out_own, 1))
    in_other = jnp.where(is_first, first_in_other, shifted(out_other, 1))
    inverse = jnp.concatenate([inverse_norm(in_own), inverse_norm(in_other)], axis=0)
    (fwd_two,) = forward(OWN, in_own, in_other, inverse, gain_rows, slopes, by_query, keep)

    grad_one = joined(first_own, grad_one_part)
    bwd_two = joined(second_own, bwd_two_part)
    return (out_own[None], grad_one[None], fwd_two[None], bwd_two[None], gain_total[None])


def solution(mesh):
    placed = (
        P("section", "seq", None),
        P("seq", None),
        P("section", "seq", None),
        P("section", "seq", None),
        P("section", "seq", None),
        P("seq", None),
        P("section", None, None),
        P("section", None),
        P(),
        P(),
    )
    return jax.shard_map(
        on_device,
        mesh=mesh,
        in_specs=placed,
        out_specs=(
            P("section", "seq", None),
            P("section", "seq", None),
            P("section", "seq", None),
            P("section", "seq", None),
            P("section", None, None),
        ),
        check_vma=False,
    )
```

time: 1060 us -> 260 us (0.25); the launches traced: 1050 us -> 258 us
  blocking collectives: 379 us -> 0 us
  matrix products: 197 us -> 0 us
  waiting for transfers between devices: 201 us -> 121 us
  local copies, waits for them, and re-layouts: 99.9 us -> 27.2 us
  other arithmetic: 81.9 us -> 15.6 us
  Pallas kernels: 0 us -> 40.1 us
  starting transfers between devices: 86.4 us -> 53.2 us
    psum x1 -> x0, blocking collectives: 379 us -> none  [summed(): return lax.psum(gain_part, 'seq')]
    dot_general x14 -> x0, matrix products: 197 us -> none  [product(): jnp.einsum(einsum_form, left, right, preferred_element_type=jnp.float32)]
    all_to_all x10 -> x0, waiting for transfers between devices: 171 us -> none  [the longest x4 81 us: to_heads(): lax.all_to_all(blocks, 'seq', split_axis=0, concat_axis=0, tiled=True)]
    ppermute x2 -> x23, waiting for transfers between devices: 29.8 us -> 121 us  [the longest x10 114 us: swap(): return lax.ppermute(value, 'seq', partners)]
    all_to_all x10 -> x0, starting transfers between devices: 82.6 us -> none  [the longest x4 27.8 us: to_heads(): lax.all_to_all(blocks, 'seq', split_axis=0, concat_axis=0, tiled=True)]
    ppermute x2 -> x23, starting transfers between devices: 3.82 us -> 53.2 us  [the longest x10 22.4 us: swap(): return lax.ppermute(value, 'seq', partners)]
    convert_element_type x20 -> x1, other arithmetic: 47.9 us -> 0.91 us  [on_device(): keep = wet.astype(jnp.float32)[:, None]]
    pallas_call x0 -> x6, Pallas kernels: none -> 40.1 us  [the longest x2 18.8 us: backward(): pl.pallas_call(functools.partial(backward_body, STEP_HEADS), grid_spec=pl...]
  transfers between devices with their start and end apart: 12 -> 23, of which waited for: 10 -> 10; matrix products, arithmetic and copies ran while one was open for 14% -> 9% of each run, Pallas kernels for 0% -> 4%
where the time goes in v1:
time: 260 us; the launch traced here: 258 us
  waiting for transfers between devices  121 us (47%)
  starting transfers between devices  53.2 us (20%)
  Pallas kernels  40.1 us (15%)
  local copies, waits for them, and re-layouts  27.2 us (10%)
  other arithmetic  15.6 us (6%)
    ppermute x10, waiting for transfers between devices, swap(): return lax.ppermute(value, 'seq', partners)  114 us
    ppermute x10, starting transfers between devices, swap(): return lax.ppermute(value, 'seq', partners)  22.4 us
    unnamed x58, local copies, waits for them, and re-layouts  19 us
    pallas_call x2, Pallas kernels, backward(): pl.pallas_call(functools.partial(backward_body, STEP_HEADS), grid_spec=pl...  18.8 us
    ppermute x7, starting transfers between devices, on_device(): lax.ppermute(gain, 'seq', [(i, i ^ flip) for i in range(devices)])  15.4 us
    pallas_call x2, Pallas kernels, forward(): pl.pallas_call(functools.partial(forward_body, query_rows, STEP_HEADS), g...  13.8 us
    ppermute x4, starting transfers between devices, shifted(): lax.ppermute(value, 'section', [(s, s + steps) for s in range(first, last)])  13.1 us
    pallas_call x2, Pallas kernels, combine(): pl.pallas_call(combine_body, grid_spec=pltpu.PrefetchScalarGridSpec(num_s...  7.59 us
  transfers between devices with their start and end apart: 23, of which 10 were waited for; matrix products, arithmetic and copies ran while one was open for 9% of the time, Pallas kernels for 4%

profile of v1, /device:TPU:32, one launch (start us, length us, event | category | flops | bytes accessed | tf_op | source)
XLA Modules:
  0.0 258.5 jit_solution(12919826232929251122)
XLA Ops:
  2.7 3.3 %collective-permute-start = (bf16[128,2048]{1,0:T(8,128)(2,1)}, bf16[128,2048]{1,0:T(8,128)(2,1)}, u32[]{:S(2)}, u32[]{:S(2)}) collective-permute-start(bf16[128,2048]{1,0:T(8,128)(2,1)} %dynamic-slice_bitcast_fusion.1), channel_id=1, source_target_pairs={{0,1},{1,0},{2,3},{3,2},{4,5},{5,4},{6,7},{7,6},{8,9},{9,8},{10,11... | collective-permute-start | bytes 1572872 | tf_op jit(solution)/shard_map/ppermute | solution.py:271
  8.6 2.9 %collective-permute-start.4 = (f32[128,2]{0,1:T(2,128)S(1)}, f32[128,2]{0,1:T(2,128)}, u32[]{:S(2)}, u32[]{:S(2)}) collective-permute-start(f32[128,2]{0,1:T(2,128)S(1)} %pad_maximum_fusion.2), channel_id=1, source_target_pairs={{0,1},{1,0},{2,3},{3,2},{4,5},{5,4},{6,7},{7,6},{8,9},{9,8},{10,11... | collective-permute-start | bytes 3080 | tf_op jit(solution)/shard_map/ppermute | solution.py:271
  17.1 33.6 %collective-permute-done.4 = f32[128,2]{0,1:T(2,128)} collective-permute-done((f32[128,2]{0,1:T(2,128)S(1)}, f32[128,2]{0,1:T(2,128)}, u32[]{:S(2)}, u32[]{:S(2)}) %collective-permute-start.4) | collective-permute-done | bytes 1056 | tf_op jit(solution)/shard_map/ppermute | solution.py:271
  55.0 9.1 %differentiate.2 = (f32[256,2048]{1,0:T(8,128)S(1)}, f32[3,2048]{1,0:T(4,128)S(1)}, f32[256,1]{1,0:T(8,128)S(1)}) custom-call(s32[1]{0:T(128)} %bitcast.10.side_ref, bf16[128,4096]{1,0:T(8,128)(2,1)S(1)} %bitcast.43, bf16[128,2048]{1,0:T(8,128)(2,1)} %collective-permute-done.other_ref, bf16[128,4096]{1,0:T(8,128)(2,1)S(1)} %bitcast.45, ...), custom_call_target="tpu_custom_call" | custom-call | flops 1342177280 | bytes 4194304 | tf_op jit(solution)/shard_map/differentiate/pallas_call | solution.py:159
  65.4 3.4 %collective-permute-start.5 = (f32[256,1]{1,0:T(8,128)S(1)}, f32[256,1]{1,0:T(8,128)S(1)}, u32[]{:S(2)}, u32[]{:S(2)}) collective-permute-start(f32[256,1]{1,0:T(8,128)S(1)} %get-tuple-element.27), channel_id=1, source_target_pairs={{0,1},{1,0},{2,3},{3,2},{4,5},{5,4},{6,7},{7,6},{8,9},{9,8},{10,11... | collective-permute-start | bytes 3080 | tf_op jit(solution)/shard_map/ppermute | solution.py:271
  68.8 3.7 %collective-permute-done.5 = f32[256,1]{1,0:T(8,128)S(1)} collective-permute-done((f32[256,1]{1,0:T(8,128)S(1)}, f32[256,1]{1,0:T(8,128)S(1)}, u32[]{:S(2)}, u32[]{:S(2)}) %collective-permute-start.5) | collective-permute-done | bytes 1056 | tf_op jit(solution)/shard_map/ppermute | solution.py:271
  72.6 4.0 %combine.2 = (bf16[128,2048]{1,0:T(8,128)(2,1)}, bf16[128,2048]{1,0:T(8,128)(2,1)S(1)}) custom-call(s32[1]{0:T(128)} %bitcast.10.side_ref, bf16[128,4096]{1,0:T(8,128)(2,1)S(1)} %bitcast.44, bf16[128,2048]{1,0:T(8,128)(2,1)} %collective-permute-done.other_ref, bf16[128,4096]{1,0:T(8,128)(2,1)S(1)} %bitcast.46, ...), custom_call_target="tpu_custom_call" | custom-call | flops 3145728 | bytes 5242880 | tf_op jit(solution)/shard_map/combine/pallas_call | solution.py:223
  79.5 4.8 %collective-permute-start.12 = (bf16[128,2048]{1,0:T(8,128)(2,1)}, bf16[128,2048]{1,0:T(8,128)(2,1)S(1)}, u32[]{:S(2)}, u32[]{:S(2)}) collective-permute-start(bf16[128,2048]{1,0:T(8,128)(2,1)} %copy-done.23), channel_id=1, source_target_pairs={{64,0},{128,64},{192,128},{65,1},{129,65},{193,129},{66,2},{130,66... | collective-permute-start | bytes 1572872 | tf_op jit(solution)/shard_map/ppermute | solution.py:281
  96.7 15.9 %collective-permute-done.1.other_ref = bf16[128,2048]{1,0:T(8,128)(2,1)} collective-permute-done((bf16[128,2048]{1,0:T(8,128)(2,1)}, bf16[128,2048]{1,0:T(8,128)(2,1)}, u32[]{:S(2)}, u32[]{:S(2)}) %collective-permute-start.1) | collective-permute-done | bytes 524320 | tf_op jit(solution)/shard_map/ppermute | solution.py:271
  115.2 9.7 %differentiate.3 = (f32[256,2048]{1,0:T(8,128)S(1)}, f32[3,2048]{1,0:T(4,128)S(1)}, f32[256,1]{1,0:T(8,128)}) custom-call(s32[1]{0:T(128)} %bitcast.10.side_ref, bf16[128,4096]{1,0:T(8,128)(2,1)S(1)} %bitcast.41, bf16[128,2048]{1,0:T(8,128)(2,1)} %collective-permute-done.1.other_ref, bf16[128,2048]{1,0:T(8,128)(2,1)S(1)} %get-tuple-element.61.cot_own_ref, ...), custom_call_target="tpu_custom_call" | custom-call | flops 1342177280 | bytes 4194304 | tf_op jit(solution)/shard_map/differentiate/pallas_call | solution.py:159
  126.9 5.9 %collective-permute-start.15 = (f32[3,2048]{1,0:T(4,128)}, f32[3,2048]{1,0:T(4,128)}, u32[]{:S(2)}, u32[]{:S(2)}) collective-permute-start(f32[3,2048]{1,0:T(4,128)} %add.145), channel_id=1, source_target_pairs={{0,2},{1,3},{2,0},{3,1},{4,6},{5,7},{6,4},{7,5},{8,10},{9,11},{10,... | collective-permute-start | bytes 73736 | tf_op jit(solution)/shard_map/ppermute | solution.py:349
  132.7 3.4 %collective-permute-start.13 = (f32[256,1]{1,0:T(8,128)}, f32[256,1]{1,0:T(8,128)}, u32[]{:S(2)}, u32[]{:S(2)}) collective-permute-start(f32[256,1]{1,0:T(8,128)} %get-tuple-element.35), channel_id=1, source_target_pairs={{0,1},{1,0},{2,3},{3,2},{4,5},{5,4},{6,7},{7,6},{8,9},{9,8},{10,11... | collective-permute-start | bytes 3080 | tf_op jit(solution)/shard_map/ppermute | solution.py:271
  138.5 2.7 %collective-permute-start.17 = (f32[3,2048]{1,0:T(4,128)S(1)}, f32[3,2048]{1,0:T(4,128)S(1)}, u32[]{:S(2)}, u32[]{:S(2)}) collective-permute-start(f32[3,2048]{1,0:T(4,128)S(1)} %add.146), channel_id=1, source_target_pairs={{0,8},{1,9},{2,10},{3,11},{4,12},{5,13},{6,14},{7,15},{8,0},{9,1},... | collective-permute-start | bytes 73736 | tf_op jit(solution)/shard_map/ppermute | solution.py:349
  148.1 2.9 %collective-permute-start.20 = (f32[3,2048]{1,0:T(4,128)S(1)}, f32[3,2048]{1,0:T(4,128)S(1)}, u32[]{:S(2)}, u32[]{:S(2)}) collective-permute-start(f32[3,2048]{1,0:T(4,128)S(1)} %add_add_fusion.1), channel_id=1, source_target_pairs={{0,32},{1,33},{2,34},{3,35},{4,36},{5,37},{6,38},{7,39},{8,40},{9,... | collective-permute-start | bytes 73736 | tf_op jit(solution)/shard_map/ppermute | solution.py:349
  154.6 3.6 %combine.3 = (bf16[128,2048]{1,0:T(8,128)(2,1)S(1)}, bf16[128,2048]{1,0:T(8,128)(2,1)}) custom-call(s32[1]{0:T(128)} %bitcast.10.side_ref, bf16[128,4096]{1,0:T(8,128)(2,1)S(1)} %bitcast.42, bf16[128,2048]{1,0:T(8,128)(2,1)} %collective-permute-done.1.other_ref, bf16[128,2048]{1,0:T(8,128)(2,1)S(1)} %get-tuple-element.61.cot_own_ref, ...), custom_call_target="tpu_custom_call" | custom-call | flops 3145728 | bytes 5242880 | tf_op jit(solution)/shard_map/combine/pallas_call | solution.py:223
  158.3 3.0 %collective-permute-start.22 = (f32[3,2048]{1,0:T(4,128)S(1)}, f32[3,2048]{1,0:T(4,128)S(1)}, u32[]{:S(2)}, u32[]{:S(2)}) collective-permute-start(f32[3,2048]{1,0:T(4,128)S(1)} %add_add_fusion), channel_id=1, source_target_pairs={{0,1},{1,0},{2,3},{3,2},{4,5},{5,4},{6,7},{7,6},{8,9},{9,8},{10,11... | collective-permute-start | bytes 73736 | tf_op jit(solution)/shard_map/ppermute | solution.py:271
  161.2 25.9 %collective-permute-done.2.other_ref = bf16[128,4096]{1,0:T(8,128)(2,1)S(1)} collective-permute-done((bf16[128,4096]{1,0:T(8,128)(2,1)S(1)}, bf16[128,4096]{1,0:T(8,128)(2,1)S(1)}, u32[]{:S(2)}, u32[]{:S(2)}) %collective-permute-start.2) | collective-permute-done | bytes 1048608 | tf_op jit(solution)/shard_map/ppermute | solution.py:271
  187.1 3.4 %collective-permute-start.14 = (bf16[128,2048]{1,0:T(8,128)(2,1)}, bf16[128,2048]{1,0:T(8,128)(2,1)}, u32[]{:S(2)}, u32[]{:S(2)}) collective-permute-start(bf16[128,2048]{1,0:T(8,128)(2,1)} %get-tuple-element.38), channel_id=1, source_target_pairs={{0,1},{1,0},{2,3},{3,2},{4,5},{5,4},{6,7},{7,6},{8,9},{9,8},{10,11... | collective-permute-start | bytes 1572872 | tf_op jit(solution)/shard_map/ppermute | solution.py:271
  194.0 7.4 %attend256.1 = (bf16[128,4096]{1,0:T(8,128)(2,1)}, bf16[128,4096]{1,0:T(8,128)(2,1)S(1)}) custom-call(bf16[128,4096]{1,0:T(8,128)(2,1)S(1)} %bitcast.48, bf16[128,4096]{1,0:T(8,128)(2,1)S(1)} %copy-done.8, f32[256,1]{1,0:T(8,128)S(1)} %copy.37.inverse_ref, f32[3,4096]{1,0:T(4,128)S(1)} %bitcast.52, f32[1,32]{1,0:T(1,128)S(1)} %copy-done.22, ...), custom_call_target="tpu_custom_call" | custom-call | flops 1073741824 | bytes 6291456 | tf_op jit(solution)/shard_map/attend256/pallas_call | solution.py:67
  201.4 4.4 %collective-permute-start.7 = (bf16[128,4096]{1,0:T(8,128)(2,1)}, bf16[128,4096]{1,0:T(8,128)(2,1)S(1)}, u32[]{:S(2)}, u32[]{:S(2)}) collective-permute-start(bf16[128,4096]{1,0:T(8,128)(2,1)} %get-tuple-element.25), channel_id=1, source_target_pairs={{0,64},{64,128},{128,192},{1,65},{65,129},{129,193},{2,66},{66,130... | collective-permute-start | bytes 3145736 | tf_op jit(solution)/shard_map/ppermute | solution.py:281
  209.6 8.1 %collective-permute-done.14 = bf16[128,2048]{1,0:T(8,128)(2,1)} collective-permute-done((bf16[128,2048]{1,0:T(8,128)(2,1)}, bf16[128,2048]{1,0:T(8,128)(2,1)}, u32[]{:S(2)}, u32[]{:S(2)}) %collective-permute-start.14) | collective-permute-done | bytes 524320 | tf_op jit(solution)/shard_map/ppermute | solution.py:271
  220.3 26.8 %collective-permute-done.6 = bf16[128,2048]{1,0:T(8,128)(2,1)S(1)} collective-permute-done((bf16[128,2048]{1,0:T(8,128)(2,1)S(1)}, bf16[128,2048]{1,0:T(8,128)(2,1)S(1)}, u32[]{:S(2)}, u32[]{:S(2)}) %collective-permute-start.6) | collective-permute-done | bytes 524320 | tf_op jit(solution)/shard_map/ppermute | solution.py:271
  247.1 2.6 %maximum_select_fusion = bf16[1,128,4096]{2,1,0:T(8,128)(2,1)} fusion(bf16[1,128,2048]{2,1,0:T(8,128)(2,1)S(1)} %bitcast.55, bf16[1,128,2048]{2,1,0:T(8,128)(2,1)} %bitcast.17, pred[]{:T(512)S(6)} %eq.13), kind=kLoop, calls=%fused_computation.6 | loop fusion | flops 4718592 | bytes 2097153 | tf_op jit(solution)/shard_map/jit(_where)/select_n | solution.py:292
  252.1 6.3 %attend128.1 = bf16[128,4096]{1,0:T(8,128)(2,1)} custom-call(bf16[128,4096]{1,0:T(8,128)(2,1)S(1)} %get-tuple-element.57.own_ref, bf16[128,4096]{1,0:T(8,128)(2,1)S(1)} %get-tuple-element.59.other_ref, f32[256,1]{1,0:T(8,128)S(1)} %copy.39.inverse_ref, f32[3,4096]{1,0:T(4,128)S(1)} %bitcast.53, f32[1,32]{1,0:T(1,128)S(1)} %copy-done.22, ...), custom_call_target="tpu_custom_call" | custom-call | flops 536870912 | bytes 4194304 | tf_op jit(solution)/shard_map/attend128/pallas_call | solution.py:67
  (128 shorter events, 60.6 us)
Async XLA Ops:
  2.7 49.5 %copy-start.22 = (f32[1,32]{1,0:T(1,128)S(1)}, f32[1,32]{1,0:T(1,128)}, u32[]{:S(2)}) copy-start(f32[1,32]{1,0:T(1,128)} %slopes_ref.7) | copy-start | bytes 388
  2.7 49.5 %collective-permute-start = (bf16[128,2048]{1,0:T(8,128)(2,1)}, bf16[128,2048]{1,0:T(8,128)(2,1)}, u32[]{:S(2)}, u32[]{:S(2)}) collective-permute-start(bf16[128,2048]{1,0:T(8,128)(2,1)} %dynamic-slice_bitcast_fusion.1), channel_id=1, source_target_pairs={{0,1},{1,0},{2,3},{3,2},{4,5},{5,4},{6,7},{7,6},{8,9},{9,8},{10,11... | collective-permute-start | bytes 1572872 | tf_op jit(solution)/shard_map/ppermute | solution.py:271
  7.9 44.4 %collective-permute-start.3 = (bf16[128,2048]{1,0:T(8,128)(2,1)}, bf16[128,2048]{1,0:T(8,128)(2,1)}, u32[]{:S(2)}, u32[]{:S(2)}) collective-permute-start(bf16[128,2048]{1,0:T(8,128)(2,1)} %dynamic-slice_bitcast_fusion), channel_id=1, source_target_pairs={{0,1},{1,0},{2,3},{3,2},{4,5},{5,4},{6,7},{7,6},{8,9},{9,8},{10,11... | collective-permute-start | bytes 1572872 | tf_op jit(solution)/shard_map/ppermute | solution.py:271
  8.6 42.2 %collective-permute-start.4 = (f32[128,2]{0,1:T(2,128)S(1)}, f32[128,2]{0,1:T(2,128)}, u32[]{:S(2)}, u32[]{:S(2)}) collective-permute-start(f32[128,2]{0,1:T(2,128)S(1)} %pad_maximum_fusion.2), channel_id=1, source_target_pairs={{0,1},{1,0},{2,3},{3,2},{4,5},{5,4},{6,7},{7,6},{8,9},{9,8},{10,11... | collective-permute-start | bytes 3080 | tf_op jit(solution)/shard_map/ppermute | solution.py:271
  65.4 7.2 %collective-permute-start.5 = (f32[256,1]{1,0:T(8,128)S(1)}, f32[256,1]{1,0:T(8,128)S(1)}, u32[]{:S(2)}, u32[]{:S(2)}) collective-permute-start(f32[256,1]{1,0:T(8,128)S(1)} %get-tuple-element.27), channel_id=1, source_target_pairs={{0,1},{1,0},{2,3},{3,2},{4,5},{5,4},{6,7},{7,6},{8,9},{9,8},{10,11... | collective-permute-start | bytes 3080 | tf_op jit(solution)/shard_map/ppermute | solution.py:271
  77.4 9.0 %collective-permute-start.10 = (bf16[128,2048]{1,0:T(8,128)(2,1)}, bf16[128,2048]{1,0:T(8,128)(2,1)}, u32[]{:S(2)}, u32[]{:S(2)}) collective-permute-start(bf16[128,2048]{1,0:T(8,128)(2,1)} %get-tuple-element.28), channel_id=1, source_target_pairs={{64,0},{128,64},{192,128},{65,1},{129,65},{193,129},{66,2},{130,66... | collective-permute-start | bytes 1572872 | tf_op jit(solution)/shard_map/ppermute | solution.py:281
  79.5 15.3 %collective-permute-start.12 = (bf16[128,2048]{1,0:T(8,128)(2,1)}, bf16[128,2048]{1,0:T(8,128)(2,1)S(1)}, u32[]{:S(2)}, u32[]{:S(2)}) collective-permute-start(bf16[128,2048]{1,0:T(8,128)(2,1)} %copy-done.23), channel_id=1, source_target_pairs={{64,0},{128,64},{192,128},{65,1},{129,65},{193,129},{66,2},{130,66... | collective-permute-start | bytes 1572872 | tf_op jit(solution)/shard_map/ppermute | solution.py:281
  88.8 6.8 %collective-permute-start.11 = (bf16[128,2048]{1,0:T(8,128)(2,1)}, bf16[128,2048]{1,0:T(8,128)(2,1)}, u32[]{:S(2)}, u32[]{:S(2)}) collective-permute-start(bf16[128,2048]{1,0:T(8,128)(2,1)} %get-tuple-element.33), channel_id=1, source_target_pairs={{192,193},{193,192},{194,195},{195,194},{196,197},{197,196},{198,1... | collective-permute-start | bytes 1572872 | tf_op jit(solution)/shard_map/ppermute | solution.py:275
  91.1 21.5 %collective-permute-start.1 = (bf16[128,2048]{1,0:T(8,128)(2,1)}, bf16[128,2048]{1,0:T(8,128)(2,1)}, u32[]{:S(2)}, u32[]{:S(2)}) collective-permute-start(bf16[128,2048]{1,0:T(8,128)(2,1)} %dynamic-slice_bitcast_fusion.2), channel_id=1, source_target_pairs={{0,1},{1,0},{2,3},{3,2},{4,5},{5,4},{6,7},{7,6},{8,9},{9,8},{10,11... | collective-permute-start | bytes 1572872 | tf_op jit(solution)/shard_map/ppermute | solution.py:271
  126.9 9.3 %collective-permute-start.15 = (f32[3,2048]{1,0:T(4,128)}, f32[3,2048]{1,0:T(4,128)}, u32[]{:S(2)}, u32[]{:S(2)}) collective-permute-start(f32[3,2048]{1,0:T(4,128)} %add.145), channel_id=1, source_target_pairs={{0,2},{1,3},{2,0},{3,1},{4,6},{5,7},{6,4},{7,5},{8,10},{9,11},{10,... | collective-permute-start | bytes 73736 | tf_op jit(solution)/shard_map/ppermute | solution.py:349
  132.7 9.0 %collective-permute-start.13 = (f32[256,1]{1,0:T(8,128)}, f32[256,1]{1,0:T(8,128)}, u32[]{:S(2)}, u32[]{:S(2)}) collective-permute-start(f32[256,1]{1,0:T(8,128)} %get-tuple-element.35), channel_id=1, source_target_pairs={{0,1},{1,0},{2,3},{3,2},{4,5},{5,4},{6,7},{7,6},{8,9},{9,8},{10,11... | collective-permute-start | bytes 3080 | tf_op jit(solution)/shard_map/ppermute | solution.py:271
  136.1 51.0 %collective-permute-start.2 = (bf16[128,4096]{1,0:T(8,128)(2,1)S(1)}, bf16[128,4096]{1,0:T(8,128)(2,1)S(1)}, u32[]{:S(2)}, u32[]{:S(2)}) collective-permute-start(bf16[128,4096]{1,0:T(8,128)(2,1)S(1)} %bitcast.47), channel_id=1, source_target_pairs={{0,1},{1,0},{2,3},{3,2},{4,5},{5,4},{6,7},{7,6},{8,9},{9,8},{10,11... | collective-permute-start | bytes 3145736 | tf_op jit(solution)/shard_map/ppermute | solution.py:271
  136.9 5.7 %collective-permute-start.16 = (f32[3,2048]{1,0:T(4,128)S(1)}, f32[3,2048]{1,0:T(4,128)S(1)}, u32[]{:S(2)}, u32[]{:S(2)}) collective-permute-start(f32[3,2048]{1,0:T(4,128)S(1)} %add.146), channel_id=1, source_target_pairs={{0,4},{1,5},{2,6},{3,7},{4,0},{5,1},{6,2},{7,3},{8,12},{9,13},{10,... | collective-permute-start | bytes 73736 | tf_op jit(solution)/shard_map/ppermute | solution.py:349
  138.5 5.4 %collective-permute-start.17 = (f32[3,2048]{1,0:T(4,128)S(1)}, f32[3,2048]{1,0:T(4,128)S(1)}, u32[]{:S(2)}, u32[]{:S(2)}) collective-permute-start(f32[3,2048]{1,0:T(4,128)S(1)} %add.146), channel_id=1, source_target_pairs={{0,8},{1,9},{2,10},{3,11},{4,12},{5,13},{6,14},{7,15},{8,0},{9,1},... | collective-permute-start | bytes 73736 | tf_op jit(solution)/shard_map/ppermute | solution.py:349
  141.3 5.1 %collective-permute-start.18 = (f32[3,2048]{1,0:T(4,128)S(1)}, f32[3,2048]{1,0:T(4,128)S(1)}, u32[]{:S(2)}, u32[]{:S(2)}) collective-permute-start(f32[3,2048]{1,0:T(4,128)S(1)} %add.146), channel_id=1, source_target_pairs={{0,12},{1,13},{2,14},{3,15},{4,8},{5,9},{6,10},{7,11},{8,4},{9,5},... | collective-permute-start | bytes 73736 | tf_op jit(solution)/shard_map/ppermute | solution.py:349
  146.4 11.8 %collective-permute-start.19 = (f32[3,2048]{1,0:T(4,128)S(1)}, f32[3,2048]{1,0:T(4,128)S(1)}, u32[]{:S(2)}, u32[]{:S(2)}) collective-permute-start(f32[3,2048]{1,0:T(4,128)S(1)} %add_add_fusion.1), channel_id=1, source_target_pairs={{0,16},{1,17},{2,18},{3,19},{4,20},{5,21},{6,22},{7,23},{8,24},{9,... | collective-permute-start | bytes 73736 | tf_op jit(solution)/shard_map/ppermute | solution.py:349
  148.1 10.1 %collective-permute-start.20 = (f32[3,2048]{1,0:T(4,128)S(1)}, f32[3,2048]{1,0:T(4,128)S(1)}, u32[]{:S(2)}, u32[]{:S(2)}) collective-permute-start(f32[3,2048]{1,0:T(4,128)S(1)} %add_add_fusion.1), channel_id=1, source_target_pairs={{0,32},{1,33},{2,34},{3,35},{4,36},{5,37},{6,38},{7,39},{8,40},{9,... | collective-permute-start | bytes 73736 | tf_op jit(solution)/shard_map/ppermute | solution.py:349
  151.0 7.2 %collective-permute-start.21 = (f32[3,2048]{1,0:T(4,128)S(1)}, f32[3,2048]{1,0:T(4,128)S(1)}, u32[]{:S(2)}, u32[]{:S(2)}) collective-permute-start(f32[3,2048]{1,0:T(4,128)S(1)} %add_add_fusion.1), channel_id=1, source_target_pairs={{0,48},{1,49},{2,50},{3,51},{4,52},{5,53},{6,54},{7,55},{8,56},{9,... | collective-permute-start | bytes 73736 | tf_op jit(solution)/shard_map/ppermute | solution.py:349
  158.3 48.0 %collective-permute-start.22 = (f32[3,2048]{1,0:T(4,128)S(1)}, f32[3,2048]{1,0:T(4,128)S(1)}, u32[]{:S(2)}, u32[]{:S(2)}) collective-permute-start(f32[3,2048]{1,0:T(4,128)S(1)} %add_add_fusion), channel_id=1, source_target_pairs={{0,1},{1,0},{2,3},{3,2},{4,5},{5,4},{6,7},{7,6},{8,9},{9,8},{10,11... | collective-permute-start | bytes 73736 | tf_op jit(solution)/shard_map/ppermute | solution.py:271
  187.1 30.6 %collective-permute-start.14 = (bf16[128,2048]{1,0:T(8,128)(2,1)}, bf16[128,2048]{1,0:T(8,128)(2,1)}, u32[]{:S(2)}, u32[]{:S(2)}) collective-permute-start(bf16[128,2048]{1,0:T(8,128)(2,1)} %get-tuple-element.38), channel_id=1, source_target_pairs={{0,1},{1,0},{2,3},{3,2},{4,5},{5,4},{6,7},{7,6},{8,9},{9,8},{10,11... | collective-permute-start | bytes 1572872 | tf_op jit(solution)/shard_map/ppermute | solution.py:271
  201.4 48.3 %collective-permute-start.7 = (bf16[128,4096]{1,0:T(8,128)(2,1)}, bf16[128,4096]{1,0:T(8,128)(2,1)S(1)}, u32[]{:S(2)}, u32[]{:S(2)}) collective-permute-start(bf16[128,4096]{1,0:T(8,128)(2,1)} %get-tuple-element.25), channel_id=1, source_target_pairs={{0,64},{64,128},{128,192},{1,65},{65,129},{129,193},{2,66},{66,130... | collective-permute-start | bytes 3145736 | tf_op jit(solution)/shard_map/ppermute | solution.py:281
  205.8 41.3 %collective-permute-start.6 = (bf16[128,2048]{1,0:T(8,128)(2,1)S(1)}, bf16[128,2048]{1,0:T(8,128)(2,1)S(1)}, u32[]{:S(2)}, u32[]{:S(2)}) collective-permute-start(bf16[128,2048]{1,0:T(8,128)(2,1)S(1)} %copy-done.24), channel_id=1, source_target_pairs={{0,1},{1,0},{2,3},{3,2},{4,5},{5,4},{6,7},{7,6},{8,9},{9,8},{10,11... | collective-permute-start | bytes 1572872 | tf_op jit(solution)/shard_map/ppermute | solution.py:271
  206.9 44.6 %collective-permute-start.9 = (bf16[128,4096]{1,0:T(8,128)(2,1)S(1)}, bf16[128,4096]{1,0:T(8,128)(2,1)S(1)}, u32[]{:S(2)}, u32[]{:S(2)}) collective-permute-start(bf16[128,4096]{1,0:T(8,128)(2,1)S(1)} %get-tuple-element.32), channel_id=1, source_target_pairs={{0,64},{64,128},{128,192},{1,65},{65,129},{129,193},{2,66},{66,130... | collective-permute-start | bytes 3145736 | tf_op jit(solution)/shard_map/ppermute | solution.py:281
  208.8 42.7 %collective-permute-start.8 = (bf16[128,4096]{1,0:T(8,128)(2,1)S(1)}, bf16[128,4096]{1,0:T(8,128)(2,1)S(1)}, u32[]{:S(2)}, u32[]{:S(2)}) collective-permute-start(bf16[128,4096]{1,0:T(8,128)(2,1)S(1)} %copy-done.25), channel_id=1, source_target_pairs={{0,1},{1,0},{2,3},{3,2},{4,5},{5,4},{6,7},{7,6},{8,9},{9,8},{10,11... | collective-permute-start | bytes 3145736 | tf_op jit(solution)/shard_map/ppermute | solution.py:275
  (26 other events, 206.6 us)

commit v2 on v1

v2 whole, which is shorter than its diff:
```python
import functools

import jax
import jax.numpy as jnp
from jax import lax
from jax.experimental import pallas as pl
from jax.experimental.pallas import tpu as pltpu
from jax.sharding import PartitionSpec as P

D = 4096
HEADS = 32
HD = 128
REGION = 256
OWN = 128
HALF = D // 2
LATE = 3 * D // 4
LOG2E = 1.4426950408889634
SCALE = HD ** (-0.5)
FAR = 1e30
STEP_HEADS = 4
VMEM_LIMIT = 16 * 1024 * 1024
FREE = pl.CostEstimate(flops=0, bytes_accessed=0, transcendentals=0)


def dot(left, right, left_dim, right_dim):
    return lax.dot_general(
        left,
        right,
        (((left_dim,), (right_dim,)), ((), ())),
        preferred_element_type=jnp.float32,
    )


def columns_of(rows_ref, out_ref):
    for part in range(2):
        row = jnp.broadcast_to(rows_ref[part : part + 1, :OWN], (OWN, OWN))
        out_ref[part * OWN : (part + 1) * OWN] = jnp.transpose(row)


def split_columns(refs, out_ref):
    for part, ref in enumerate(refs):
        pieces = ref[:, 0:3].astype(jnp.float32)
        column = (pieces[:, 0:1] + pieces[:, 1:2]) + pieces[:, 2:3]
        out_ref[part * OWN : (part + 1) * OWN] = jnp.broadcast_to(column, (OWN, HD))


def rows_of(own_ref, other_ref, cols):
    return jnp.concatenate([own_ref[:, cols], other_ref[:, cols]], axis=0).astype(jnp.float32)


def row_block(array, part, width, column):
    row = part if array.shape[0] == REGION else 0
    return pl.BlockSpec((OWN, width), lambda j, *s: (row, column(j, *s)))


def whole(shape):
    return pl.BlockSpec(shape, lambda j, *s: (0, 0))


def forward_body(
    query_rows, heads, own_ref, other_ref, inverse_ref, gains_ref, slopes_ref, table_ref, keep_ref, *refs
):
    *out_refs, column_ref = refs
    step = pl.program_id(0)

    @pl.when(step == 0)
    def _():
        columns_of(inverse_ref, column_ref)

    inverse = column_ref[...]
    keep = keep_ref[:query_rows]
    ones = jnp.ones((REGION, HD), jnp.bfloat16)
    for head in range(heads):
        cols = pl.ds(head * HD, HD)
        gains = gains_ref[:, cols]
        hidden = rows_of(own_ref, other_ref, cols)
        normed_in = (hidden * inverse).astype(jnp.bfloat16).astype(jnp.float32)
        query = (normed_in[:query_rows] * gains[0:1]).astype(jnp.bfloat16)
        key = (normed_in * gains[1:2]).astype(jnp.bfloat16)
        value = (normed_in * gains[2:3]).astype(jnp.bfloat16)
        slope = slopes_ref[0, step * heads + head] * LOG2E
        scores = dot(query, key, 1, 1) * (SCALE * LOG2E) - slope * table_ref[:query_rows]
        exps = jnp.exp2(scores - jnp.max(scores, axis=1, keepdims=True)).astype(jnp.bfloat16)
        mixed = dot(exps, jnp.concatenate([value, ones], axis=1), 1, 0)
        attended = (mixed[:, :HD] / mixed[:, HD:]).astype(jnp.bfloat16).astype(jnp.float32)
        result = (hidden[:query_rows] + keep * attended).astype(jnp.bfloat16)
        out_refs[0][:, cols] = result[:OWN]
        if query_rows == REGION:
            out_refs[1][:, cols] = result


def forward(query_rows, own, other, inverse, gains, slopes, table, keep):
    width = STEP_HEADS * HD
    column = lambda j: j
    rows = [OWN] if query_rows == OWN else [OWN, REGION]
    return pl.pallas_call(
        functools.partial(forward_body, query_rows, STEP_HEADS),
        grid=(D // width,),
        in_specs=[
            row_block(own, 0, width, column),
            row_block(other, 1, width, column),
            whole((2, OWN)),
            pl.BlockSpec((3, width), lambda j: (0, j)),
            pl.BlockSpec(memory_space=pltpu.SMEM),
            whole((REGION, REGION)),
            whole((REGION, 1)),
        ],
        out_specs=[pl.BlockSpec((count, width), lambda j: (0, j)) for count in rows],
        out_shape=[jax.ShapeDtypeStruct((count, D), jnp.bfloat16) for count in rows],
        scratch_shapes=[pltpu.VMEM((REGION, HD), jnp.float32)],
        compiler_params=pltpu.CompilerParams(vmem_limit_bytes=VMEM_LIMIT),
        cost_estimate=FREE,
        name="attend" + str(query_rows),
    )(own, other, inverse, gains, slopes, table, keep)


def half_blocks(steps, width, *arrays):
    here = lambda j, s: j
    within = lambda j, s: s[0] * steps + j
    return [
        row_block(array, place % 2, width, within if array.shape[1] == D else here)
        for place, array in enumerate(arrays)
    ]


def tail_blocks():
    return [pl.BlockSpec((OWN, HD), lambda j, s: (0, HALF // HD))] * 2


def backward_body(
    heads,
    side_ref,
    own_ref,
    other_ref,
    cot_own_ref,
    cot_other_ref,
    inverse_own_ref,
    inverse_other_ref,
    gains_ref,
    slopes_ref,
    table_ref,
    keep_ref,
    grad_ref,
    small_ref,
    total_ref,
    column_ref,
):
    step = pl.program_id(0)
    first_head = side_ref[0] * (HEADS // 2) + step * heads
    keep = keep_ref[...]

    @pl.when(step == 0)
    def _():
        total_ref[...] = jnp.zeros_like(total_ref)
        small_ref[...] = jnp.zeros_like(small_ref)
        split_columns((inverse_own_ref, inverse_other_ref), column_ref)

    inverse = column_ref[...]

    for head in range(heads):
        cols = pl.ds(head * HD, HD)
        gains = gains_ref[:, cols]
        wide = rows_of(own_ref, other_ref, cols) * inverse
        normed_in = wide.astype(jnp.bfloat16).astype(jnp.float32)
        query = (normed_in * gains[0:1]).astype(jnp.bfloat16)
        key = (normed_in * gains[1:2]).astype(jnp.bfloat16)
        value = (normed_in * gains[2:3]).astype(jnp.bfloat16)
        masked = (rows_of(cot_own_ref, cot_other_ref, cols) * keep).astype(jnp.bfloat16)
        slope = slopes_ref[0, first_head + head] * LOG2E
        scores = dot(key, query, 1, 1) * (SCALE * LOG2E) - slope * table_ref[...]
        exps = jnp.exp2(scores - jnp.max(scores, axis=0, keepdims=True))
        probs = exps * (1.0 / jnp.sum(exps, axis=0, keepdims=True))
        grad_probs = dot(value, masked, 1, 1)
        inner = jnp.sum(probs * grad_probs, axis=0, keepdims=True)
        grad_scores = (probs * (grad_probs - inner) * SCALE).astype(jnp.bfloat16)
        grad_value = dot(probs.astype(jnp.bfloat16), masked, 1, 0)
        grad_key = dot(grad_scores, query, 1, 0)
        grad_query = dot(grad_scores, key, 0, 0)
        grad = grad_query * gains[0:1] + grad_key * gains[1:2] + grad_value * gains[2:3]
        grad_ref[:, cols] = grad
        total_ref[...] += grad * wide
        small_ref[0:1, pl.ds((step * heads + head) * HD, HD)] = jnp.sum(grad_query * normed_in, axis=0, keepdims=True)
        small_ref[1:2, pl.ds((step * heads + head) * HD, HD)] = jnp.sum(grad_key * normed_in, axis=0, keepdims=True)
        small_ref[2:3, pl.ds((step * heads + head) * HD, HD)] = jnp.sum(grad_value * normed_in, axis=0, keepdims=True)

    @pl.when(step == pl.num_programs(0) - 1)
    def _():
        moment = lax.dot_general(
            jnp.ones((8, HD), jnp.float32),
            total_ref[...],
            (((1,), (1,)), ((), ())),
            precision=lax.Precision.HIGHEST,
            preferred_element_type=jnp.float32,
        )
        small_ref[3:4, :REGION] = moment[0:1]


def backward(side, own, sent, other, cot_own, cot_other, gains, slopes, table, keep):
    width = STEP_HEADS * HD
    steps = HALF // width
    return pl.pallas_call(
        functools.partial(backward_body, STEP_HEADS),
        grid_spec=pltpu.PrefetchScalarGridSpec(
            num_scalar_prefetch=1,
            grid=(steps,),
            in_specs=[
                *half_blocks(steps, width, own, other, cot_own, cot_other),
                *tail_blocks(),
                pl.BlockSpec((3, width), lambda j, s: (0, s[0] * steps + j)),
                pl.BlockSpec(memory_space=pltpu.SMEM),
                whole((REGION, REGION)),
                whole((REGION, 1)),
            ],
            out_specs=[pl.BlockSpec((REGION, width), lambda j, s: (0, j)), whole((4, HALF))],
            scratch_shapes=[pltpu.VMEM((REGION, HD), jnp.float32)] * 2,
        ),
        out_shape=[
            jax.ShapeDtypeStruct((REGION, HALF), jnp.float32),
            jax.ShapeDtypeStruct((4, HALF), jnp.float32),
        ],
        compiler_params=pltpu.CompilerParams(vmem_limit_bytes=VMEM_LIMIT),
        cost_estimate=FREE,
        name="differentiate",
    )(side, own, other, cot_own, cot_other, sent, other, gains, slopes, table, keep)


def combine_body(
    side_ref,
    own_ref,
    other_ref,
    cot_own_ref,
    cot_other_ref,
    grad_ref,
    inverse_own_ref,
    inverse_other_ref,
    small_ref,
    received_ref,
    out_ref,
    out_other,
    column_ref,
    mean_ref,
):
    @pl.when(pl.program_id(0) == 0)
    def _():
        split_columns((inverse_own_ref, inverse_other_ref), column_ref)
        for part in range(2):
            here, there = (pl.ds(part * OWN, OWN), pl.ds((1 - part) * OWN, OWN))
            total = small_ref[3:4, here] + received_ref[3:4, there]
            mean_ref[here] = jnp.transpose(jnp.broadcast_to(total, (OWN, OWN))) * (1.0 / D)

    for part, hidden, cot in ((0, own_ref, cot_own_ref), (1, other_ref, cot_other_ref)):
        rows = pl.ds(part * OWN, OWN)
        scale = column_ref[rows]
        mean = mean_ref[rows]
        for piece in range(out_ref.shape[1] // HD):
            cols = pl.ds(piece * HD, HD)
            wide = hidden[:, cols].astype(jnp.float32) * scale
            grad = (grad_ref[rows, cols] - wide * mean) * scale
            result = (cot[:, cols].astype(jnp.float32) + grad).astype(jnp.bfloat16)
            out_ref[rows, cols] = result
            if part == 1:
                out_other[:, cols] = result


def combine(side, own, sent, other, cot_own, cot_other, grad, small, received):
    width = STEP_HEADS * HD
    steps = HALF // width
    return pl.pallas_call(
        combine_body,
        grid_spec=pltpu.PrefetchScalarGridSpec(
            num_scalar_prefetch=1,
            grid=(steps,),
            in_specs=[
                *half_blocks(steps, width, own, other, cot_own, cot_other),
                pl.BlockSpec((REGION, width), lambda j, s: (0, j)),
                *tail_blocks(),
                whole((4, HALF)),
                whole((4, HALF)),
            ],
            out_specs=[
                pl.BlockSpec((count, width), lambda j, s: (0, j)) for count in (REGION, OWN)
            ],
            scratch_shapes=[pltpu.VMEM((REGION, HD), jnp.float32)] * 2,
        ),
        out_shape=[
            jax.ShapeDtypeStruct((count, HALF), jnp.bfloat16) for count in (REGION, OWN)
        ],
        compiler_params=pltpu.CompilerParams(vmem_limit_bytes=VMEM_LIMIT),
        cost_estimate=FREE,
        name="combine",
    )(side, own, other, cot_own, cot_other, grad, sent, other, small, received)


def after(value, *earlier):
    return lax.optimization_barrier((value, earlier))[0]


def with_inverse(half, inverse):
    first = lax.reduce_precision(inverse, 8, 7)
    second = lax.reduce_precision(inverse - first, 8, 7)
    pieces = jnp.stack([first, second, inverse - first - second], axis=1).astype(jnp.bfloat16)
    return jnp.concatenate([half, jnp.pad(pieces, ((0, 0), (0, HD - 3)))], axis=1)


def inverse_norm(hidden):
    wide = hidden.astype(jnp.float32)
    return lax.rsqrt(jnp.mean(wide * wide, axis=1) + 1e-05)


def on_device(
    acts_in, first_in, saved_one, cot_one, saved_two, cot_last, gains, slopes, ocean, places
):
    devices = lax.axis_size("seq")
    sections = lax.axis_size("section")
    my_index = lax.axis_index("seq")
    section_index = lax.axis_index("section")
    side = my_index % 2
    side_vec = side.astype(jnp.int32)[None]
    acts, saved_a, cot_a, saved_b = (acts_in[0], saved_one[0], cot_one[0], saved_two[0])
    gain_rows = gains[0]

    def flips(bits):
        return [(i, i ^ bits) for i in range(devices)]

    def swap(value):
        return lax.ppermute(value, "seq", flips(1))

    def swap_in(chosen, value):
        bases = [section * devices for section in chosen]
        pairs = [(base + i, base + (i ^ 1)) for base in bases for i in range(devices)]
        return lax.ppermute(value, ("section", "seq"), pairs)

    def shifted(value, steps):
        first, last = (max(0, -steps), min(sections, sections - steps))
        return lax.ppermute(value, "section", [(s, s + steps) for s in range(first, last)])

    def for_partner(matrix):
        return lax.dynamic_slice_in_dim(matrix, (1 - side) * HALF, HALF, 1)

    def for_me(matrix):
        return lax.dynamic_slice_in_dim(matrix, side * HALF, HALF, 1)

    def joined(mine, received):
        pair = jnp.concatenate([mine, received], axis=1)
        flipped = jnp.concatenate([received, mine], axis=1)
        return jnp.where(side == 0, pair, flipped)

    def region_order(vector):
        own = lax.dynamic_slice_in_dim(vector, my_index * OWN, OWN, vector.ndim - 1)
        start = (my_index + 1 - 2 * side) * OWN
        other = lax.dynamic_slice_in_dim(vector, start, OWN, vector.ndim - 1)
        return jnp.concatenate([own, other], axis=-1)

    place = region_order(places)
    wet = region_order(ocean)
    distance = (
        jnp.abs(place[0][:, None] - place[0][None, :])
        + jnp.abs(place[1][:, None] - place[1][None, :])
    ).astype(jnp.float32)
    by_query = jnp.where(wet[None, :] > 0, distance, FAR)
    by_key = jnp.where(wet[:, None] > 0, distance, FAR)
    keep = wet.astype(jnp.float32)[:, None]

    is_first = section_index == 0
    is_last = section_index == sections - 1

    with jax.named_scope("cot_a"):
        cot_a_send = for_partner(cot_a)
        cot_a_other = swap(cot_a_send)
    with jax.named_scope("saved_a"):
        early = after(saved_a, cot_a_send)
        saved_a_sent = with_inverse(for_partner(early), inverse_norm(early))
        saved_a_other = swap(saved_a_sent)
    saved_b_sent = with_inverse(for_partner(saved_b), inverse_norm(after(saved_b, saved_a_sent)))
    with jax.named_scope("acts"):
        acts_other = swap(after(acts, saved_a_other))

    back = (side_vec, saved_a, saved_a_sent, saved_a_other, cot_a, cot_a_other)
    grad, small_a = backward(*back, gain_rows, slopes, by_key, keep)
    with jax.named_scope("small_a"):
        received_a = swap(small_a)
    received_a = after(received_a, acts_other)
    first, first_other = combine(*back, grad, small_a, received_a)
    with jax.named_scope("to_previous"):
        from_next = shifted(first, -1)
    with jax.named_scope("saved_b"):
        saved_b_other = swap(after(saved_b_sent, acts_other))
    with jax.named_scope("extra"):
        extra = jnp.concatenate([first_in[:, LATE:], for_partner(cot_last)], axis=1)
        extra = jnp.where(is_last, extra, first_in[:, :LATE])
        received_extra = swap_in((sections - 2, sections - 1), after(extra, acts_other))
    with jax.named_scope("helped"):
        early_part = lax.ppermute(received_extra, "section", [(sections - 2, 0)])
        late_part = lax.ppermute(received_extra[:, : D - LATE], "section", [(sections - 1, 0)])

    acts_other = after(acts_other, first)
    inverse = jnp.stack([inverse_norm(acts), inverse_norm(acts_other)])
    out_one, out_region = forward(
        REGION, acts, acts_other, inverse, gain_rows, slopes, by_query, keep
    )
    with jax.named_scope("to_next"):
        from_before = shifted(out_region, 1)
    with jax.named_scope("grad_one"):
        grad_one_part = swap(after(first_other, saved_b_other))

    cot_b = jnp.concatenate([for_me(cot_last), received_extra[:, D - LATE :]], axis=0)
    cot_b = after(jnp.where(is_last, cot_b, from_next), out_one)
    back = (side_vec, saved_b, saved_b_sent, saved_b_other, cot_b, cot_b)
    grad, small_b = backward(*back, gain_rows, slopes, by_key, keep)
    small = small_b + jnp.where(jnp.arange(4)[:, None] < 3, small_a, 0.0)
    with jax.named_scope("small_b"):
        received_b = swap(small)
    received_b = after(received_b, grad_one_part, early_part, late_part)
    gain_total = joined(small[:3], received_b[:3])
    received_b = after(received_b, gain_total)
    second, second_other = combine(*back, grad, small, received_b)
    with jax.named_scope("bwd_two"):
        bwd_two_part = swap(second_other)

    fed = jnp.concatenate([after(early_part, second_other), late_part], axis=1)
    fed = jnp.concatenate([first_in, fed], axis=0)
    region_in = jnp.where(is_first, fed, from_before)
    inverse = inverse_norm(region_in).reshape(2, OWN)
    (fwd_two,) = forward(OWN, region_in, region_in, inverse, gain_rows, slopes, by_query, keep)

    if devices > 2:
        with jax.named_scope("gain2"):
            gain_total = gain_total + lax.ppermute(gain_total, "seq", flips(2))
    gain_total = after(gain_total, from_before)
    for bit in (4, 16):
        if bit < devices:
            with jax.named_scope("gain" + str(bit)):
                terms = [
                    lax.ppermute(gain_total, "seq", flips(bit * flip)) for flip in range(1, 4)
                ]
            gain_total = (gain_total + terms[0]) + (terms[1] + terms[2])

    bwd_two_part = after(bwd_two_part, fwd_two, gain_total)

    grad_one = joined(first[:OWN], after(grad_one_part, second_other))
    bwd_two = joined(second[:OWN], bwd_two_part)
    return (out_one[None], grad_one[None], fwd_two[None], bwd_two[None], gain_total[None])


def solution(mesh):
    placed = (
        P("section", "seq", None),
        P("seq", None),
        P("section", "seq", None),
        P("section", "seq", None),
        P("section", "seq", None),
        P("seq", None),
        P("section", None, None),
        P("section", None),
        P(),
        P(),
    )
    return jax.shard_map(
        on_device,
        mesh=mesh,
        in_specs=placed,
        out_specs=(
            P("section", "seq", None),
            P("section", "seq", None),
            P("section", "seq", None),
            P("section", "seq", None),
            P("section", None, None),
        ),
        check_vma=False,
    )
```

time: 260 us -> 223 us (0.86); the launches traced: 258 us -> 218 us
  waiting for transfers between devices: 121 us -> 107 us
  local copies, waits for them, and re-layouts: 27.2 us -> 15.1 us
  starting transfers between devices: 53.2 us -> 45.1 us
  other arithmetic: 15.6 us -> 12.3 us
    unnamed x58 -> x32, local copies, waits for them, and re-layouts: 19 us -> 4.92 us
    ppermute x19 -> x18, waiting for transfers between devices: 118 us -> 107 us  [the longest x8 100 us: swap(): return lax.ppermute(value, 'seq', flips(1))]
    ppermute x4 -> x2, starting transfers between devices: 13.1 us -> 5.59 us  [shifted(): lax.ppermute(value, 'section', [(s, s + steps) for s in range(first, last)])]
    reduce_sum x6 -> x5, other arithmetic: 2.07 us -> 5.9 us  [inverse_norm(): return lax.rsqrt(jnp.mean(wide * wide, axis=1) + 1e-05)]
    ppermute x4 -> x2, waiting for transfers between devices: 3.5 us -> 0.01 us  [shifted(): lax.ppermute(value, 'section', [(s, s + steps) for s in range(first, last)])]
    select_n x3, other arithmetic: 5.17 us -> 2.48 us  [joined(): return jnp.where(side == 0, pair, flipped)]
    ppermute x19 -> x18, starting transfers between devices: 40 us -> 39.5 us  [the longest x8 13.9 us: swap(): return lax.ppermute(value, 'seq', flips(1))]
  transfers between devices with their start and end apart: 23 -> 20, of which waited for: 10 -> 8; matrix products, arithmetic and copies ran while one was open for 9% -> 9% of each run, Pallas kernels for 4% -> 16%
where the time goes in v2:
time: 223 us; the launch traced here: 218 us
  waiting for transfers between devices  107 us (48%)
  starting transfers between devices  45.1 us (20%)
  Pallas kernels  38 us (17%)
  local copies, waits for them, and re-layouts  15.1 us (7%)
  other arithmetic  12.3 us (6%)
    ppermute x8, waiting for transfers between devices, swap(): return lax.ppermute(value, 'seq', flips(1))  100 us
    pallas_call x2, Pallas kernels, backward(): pl.pallas_call(functools.partial(backward_body, STEP_HEADS), grid_spec=pl...  18 us
    pallas_call x2, Pallas kernels, forward(): pl.pallas_call(functools.partial(forward_body, query_rows, STEP_HEADS), g...  14.4 us
    ppermute x8, starting transfers between devices, swap(): return lax.ppermute(value, 'seq', flips(1))  13.9 us
    ppermute x1, starting transfers between devices, on_device(): gain_total = gain_total + lax.ppermute(gain_total, 'seq', flips(2))  9.05 us
    ppermute x6, starting transfers between devices, on_device(): lax.ppermute(gain_total, 'seq', flips(bit * flip))  8.36 us
    reduce_sum x5, other arithmetic, inverse_norm(): return lax.rsqrt(jnp.mean(wide * wide, axis=1) + 1e-05)  5.9 us
    ppermute x2, starting transfers between devices, shifted(): lax.ppermute(value, 'section', [(s, s + steps) for s in range(first, last)])  5.59 us
  transfers between devices with their start and end apart: 20, of which 8 were waited for; matrix products, arithmetic and copies ran while one was open for 9% of the time, Pallas kernels for 16%

profile of v2, /device:TPU:32, one launch (start us, length us, event | category | flops | bytes accessed | tf_op | source)
XLA Modules:
  0.0 218.4 jit_solution(3559551824606513229)
XLA Ops:
  0.7 2.0 dynamic-slice_bitcast_fusion.1
  2.6 3.3 %collective-permute-start.2 = (bf16[128,2048]{1,0:T(8,128)(2,1)}, bf16[128,2048]{1,0:T(8,128)(2,1)}, u32[]{:S(2)}, u32[]{:S(2)}) collective-permute-start(bf16[128,2048]{1,0:T(8,128)(2,1)} %dynamic-slice_bitcast_fusion.1), channel_id=1, source_target_pairs={{0,1},{1,0},{2,3},{3,2},{4,5},{5,4},{6,7},{7,6},{8,9},{9,8},{10,11... | collective-permute-start | bytes 1572872 | tf_op jit(solution)/shard_map/cot_a/ppermute | solution.py:326
  11.8 2.2 %constant_dynamic-slice_fusion.1 = (bf16[128,2048]{1,0:T(8,128)(2,1)}, bf16[128,2048]{1,0:T(8,128)(2,1)S(1)}) fusion(bf16[128,4096]{1,0:T(8,128)(2,1)} %param.15, s32[]{:T(128)S(6)} %select_n.102, s32[]{:T(128)S(6)} %select_n.95), kind=kLoop, calls=%fused_computation.30 | loop fusion | bytes 2097160 | tf_op jit(solution)/shard_map/dynamic_slice | solution.py:341
  14.0 38.0 %collective-permute-done.other_ref.inverse_other_ref = bf16[128,2176]{1,0:T(8,128)(2,1)S(1)} collective-permute-done((bf16[128,2176]{1,0:T(8,128)(2,1)S(1)}, bf16[128,2176]{1,0:T(8,128)(2,1)S(1)}, u32[]{:S(2)}, u32[]{:S(2)}) %collective-permute-start) | collective-permute-done | bytes 557088 | tf_op jit(solution)/shard_map/saved_a/ppermute | solution.py:326
  52.0 3.4 %collective-permute-start.1 = (bf16[128,4096]{1,0:T(8,128)(2,1)}, bf16[128,4096]{1,0:T(8,128)(2,1)}, u32[]{:S(2)}, u32[]{:S(2)}) collective-permute-start(bf16[128,4096]{1,0:T(8,128)(2,1)} %bitcast.own_ref), channel_id=1, source_target_pairs={{0,1},{1,0},{2,3},{3,2},{4,5},{5,4},{6,7},{7,6},{8,9},{9,8},{10,11... | collective-permute-start | bytes 3145736 | tf_op jit(solution)/shard_map/acts/ppermute | solution.py:326
  56.5 9.2 %differentiate.2 = (f32[256,2048]{1,0:T(8,128)S(1)}, f32[4,2048]{1,0:T(4,128)S(1)}) custom-call(s32[1]{0:T(128)} %bitcast.4.side_ref, bf16[128,4096]{1,0:T(8,128)(2,1)S(1)} %bitcast.50, bf16[128,2176]{1,0:T(8,128)(2,1)S(1)} %collective-permute-done.other_ref.inverse_other_ref, bf16[128,4096]{1,0:T(8,128)(2,1)S(1)} %bitcast.55, ...), custom_call_target="tpu_custom_call" | custom-call | tf_op jit(solution)/shard_map/differentiate/pallas_call | solution.py:201
  67.2 31.2 %collective-permute-done.3.received_ref = f32[4,2048]{1,0:T(4,128)S(1)} collective-permute-done((f32[4,2048]{1,0:T(4,128)S(1)}, f32[4,2048]{1,0:T(4,128)S(1)}, u32[]{:S(2)}, u32[]{:S(2)}) %collective-permute-start.3) | collective-permute-done | bytes 32800 | tf_op jit(solution)/shard_map/small_a/ppermute | solution.py:326
  101.2 4.0 %combine.2 = (bf16[256,2048]{1,0:T(8,128)(2,1)}, bf16[128,2048]{1,0:T(8,128)(2,1)}) custom-call(s32[1]{0:T(128)} %bitcast.4.side_ref, bf16[128,4096]{1,0:T(8,128)(2,1)S(1)} %bitcast.51, bf16[128,2176]{1,0:T(8,128)(2,1)S(1)} %collective-permute-done.other_ref.inverse_other_ref, bf16[128,4096]{1,0:T(8,128)(2,1)S(1)} %bitcast.56, ...), custom_call_target="tpu_custom_call" | custom-call | tf_op jit(solution)/shard_map/combine/pallas_call | solution.py:268
  105.2 3.0 %collective-permute-start.7 = (bf16[256,2048]{1,0:T(8,128)(2,1)}, bf16[256,2048]{1,0:T(8,128)(2,1)}, u32[]{:S(2)}, u32[]{:S(2)}) collective-permute-start(bf16[256,2048]{1,0:T(8,128)(2,1)} %get-tuple-element.35), channel_id=1, source_target_pairs={{64,0},{128,64},{192,128},{65,1},{129,65},{193,129},{66,2},{130,66... | collective-permute-start | bytes 3145736 | tf_op jit(solution)/shard_map/to_previous/ppermute | solution.py:335
  109.8 4.3 %collective-permute-start.6 = (bf16[128,3072]{1,0:T(8,128)(2,1)}, bf16[128,3072]{1,0:T(8,128)(2,1)}, u32[]{:S(2)}, u32[]{:S(2)}) collective-permute-start(bf16[128,3072]{1,0:T(8,128)(2,1)} %maximum_select_fusion.4), channel_id=1, source_target_pairs={{128,129},{129,128},{130,131},{131,130},{132,133},{133,132},{134,1... | collective-permute-start | bytes 2359304 | tf_op jit(solution)/shard_map/extra/ppermute | solution.py:331
  116.3 8.3 %attend256.1 = (bf16[128,4096]{1,0:T(8,128)(2,1)}, bf16[256,4096]{1,0:T(8,128)(2,1)S(1)}) custom-call(bf16[128,4096]{1,0:T(8,128)(2,1)} %bitcast.own_ref, bf16[128,4096]{1,0:T(8,128)(2,1)} %collective-permute-done.1.other_ref, f32[2,128]{1,0:T(2,128)S(1)} %pad_maximum_fusion.1.inverse_ref, f32[3,4096]{1,0:T(4,128)S(1)} %bitcast.58, f32[1,32]{1,0:T(1,128)S(1)} %copy-done.9, ...), custom_call_target="tpu_custom_call" | custom-call | tf_op jit(solution)/shard_map/attend256/pallas_call | solution.py:96
  124.6 2.6 %collective-permute-start.11 = (bf16[256,4096]{1,0:T(8,128)(2,1)S(1)}, bf16[256,4096]{1,0:T(8,128)(2,1)S(1)}, u32[]{:S(2)}, u32[]{:S(2)}) collective-permute-start(bf16[256,4096]{1,0:T(8,128)(2,1)S(1)} %get-tuple-element.51), channel_id=1, source_target_pairs={{0,64},{64,128},{128,192},{1,65},{65,129},{129,193},{2,66},{66,130... | collective-permute-start | bytes 6291464 | tf_op jit(solution)/shard_map/to_next/ppermute | solution.py:335
  127.2 27.4 %collective-permute-done.4.other_ref.inverse_other_ref = bf16[128,2176]{1,0:T(8,128)(2,1)S(1)} collective-permute-done((bf16[128,2176]{1,0:T(8,128)(2,1)S(1)}, bf16[128,2176]{1,0:T(8,128)(2,1)S(1)}, u32[]{:S(2)}, u32[]{:S(2)}) %collective-permute-start.4) | collective-permute-done | bytes 557088 | tf_op jit(solution)/shard_map/saved_b/ppermute | solution.py:326
  154.6 3.4 %collective-permute-start.5 = (bf16[128,2048]{1,0:T(8,128)(2,1)}, bf16[128,2048]{1,0:T(8,128)(2,1)S(1)}, u32[]{:S(2)}, u32[]{:S(2)}) collective-permute-start(bf16[128,2048]{1,0:T(8,128)(2,1)} %get-tuple-element.41), channel_id=1, source_target_pairs={{0,1},{1,0},{2,3},{3,2},{4,5},{5,4},{6,7},{7,6},{8,9},{9,8},{10,11... | collective-permute-start | bytes 1572872 | tf_op jit(solution)/shard_map/grad_one/ppermute | solution.py:326
  160.9 3.1 %collective-permute-start.9 = (bf16[128,3072]{1,0:T(8,128)(2,1)}, bf16[128,3072]{1,0:T(8,128)(2,1)S(1)}, u32[]{:S(2)}, u32[]{:S(2)}) collective-permute-start(bf16[128,3072]{1,0:T(8,128)(2,1)} %collective-permute-done.6), channel_id=1, source_target_pairs={{128,0},{129,1},{130,2},{131,3},{132,4},{133,5},{134,6},{135,7},{1... | collective-permute-start | bytes 2359304 | tf_op jit(solution)/shard_map/helped/ppermute | solution.py:393
  165.7 8.8 %differentiate.3 = (f32[256,2048]{1,0:T(8,128)S(1)}, f32[4,2048]{1,0:T(4,128)S(1)}) custom-call(s32[1]{0:T(128)} %bitcast.4.side_ref, bf16[128,4096]{1,0:T(8,128)(2,1)S(1)} %bitcast.53, bf16[128,2176]{1,0:T(8,128)(2,1)S(1)} %collective-permute-done.4.other_ref.inverse_other_ref, bf16[256,2048]{1,0:T(8,128)(2,1)S(1)} %maximum_select_fusion.1.cot_own_ref.cot_other_ref, ...), custom_call_target="tpu_custom_call" | custom-call | tf_op jit(solution)/shard_map/differentiate/pallas_call | solution.py:201
  174.5 3.0 %collective-permute-start.8 = (f32[4,2048]{1,0:T(4,128)S(1)}, f32[4,2048]{1,0:T(4,128)S(1)}, u32[]{:S(2)}, u32[]{:S(2)}) collective-permute-start(f32[4,2048]{1,0:T(4,128)S(1)} %select_add_fusion.small_ref), channel_id=1, source_target_pairs={{0,1},{1,0},{2,3},{3,2},{4,5},{5,4},{6,7},{7,6},{8,9},{9,8},{10,11... | collective-permute-start | bytes 98312 | tf_op jit(solution)/shard_map/small_b/ppermute | solution.py:326
  178.6 3.3 %collective-permute-done.5 = bf16[128,2048]{1,0:T(8,128)(2,1)S(1)} collective-permute-done((bf16[128,2048]{1,0:T(8,128)(2,1)}, bf16[128,2048]{1,0:T(8,128)(2,1)S(1)}, u32[]{:S(2)}, u32[]{:S(2)}) %collective-permute-start.5) | collective-permute-done | bytes 524320 | tf_op jit(solution)/shard_map/grad_one/ppermute | solution.py:326
  182.5 3.0 %collective-permute-done.9 = bf16[128,3072]{1,0:T(8,128)(2,1)S(1)} collective-permute-done((bf16[128,3072]{1,0:T(8,128)(2,1)}, bf16[128,3072]{1,0:T(8,128)(2,1)S(1)}, u32[]{:S(2)}, u32[]{:S(2)}) %collective-permute-start.9) | collective-permute-done | bytes 786464 | tf_op jit(solution)/shard_map/helped/ppermute | solution.py:393
  185.4 9.1 %collective-permute-start.13 = (f32[3,4096]{1,0:T(4,128)S(1)}, f32[3,4096]{1,0:T(4,128)S(1)}, u32[]{:S(2)}, u32[]{:S(2)}) collective-permute-start(f32[3,4096]{1,0:T(4,128)S(1)} %maximum_select_fusion.5), channel_id=1, source_target_pairs={{0,2},{1,3},{2,0},{3,1},{4,6},{5,7},{6,4},{7,5},{8,10},{9,11},{10,... | collective-permute-start | bytes 147464 | tf_op jit(solution)/shard_map/gain2/ppermute | solution.py:428
  197.5 2.8 %collective-permute-start.16 = (f32[3,4096]{1,0:T(4,128)S(1)}, f32[3,4096]{1,0:T(4,128)S(1)}, u32[]{:S(2)}, u32[]{:S(2)}) collective-permute-start(f32[3,4096]{1,0:T(4,128)S(1)} %add.138), channel_id=1, source_target_pairs={{0,12},{1,13},{2,14},{3,15},{4,8},{5,9},{6,10},{7,11},{8,4},{9,5},... | collective-permute-start | bytes 147464 | tf_op jit(solution)/shard_map/gain4/ppermute | solution.py:434
  203.0 3.1 %collective-permute-done.15 = f32[3,4096]{1,0:T(4,128)S(1)} collective-permute-done((f32[3,4096]{1,0:T(4,128)S(1)}, f32[3,4096]{1,0:T(4,128)S(1)}, u32[]{:S(2)}, u32[]{:S(2)}) %collective-permute-start.15) | collective-permute-done | bytes 49184 | tf_op jit(solution)/shard_map/gain4/ppermute | solution.py:434
  206.1 3.1 %collective-permute-start.19 = (f32[3,4096]{1,0:T(4,128)S(1)}, f32[3,4096]{1,0:T(4,128)S(1)}, u32[]{:S(2)}, u32[]{:S(2)}) collective-permute-start(f32[3,4096]{1,0:T(4,128)S(1)} %add_add_fusion.1), channel_id=1, source_target_pairs={{0,48},{1,49},{2,50},{3,51},{4,52},{5,53},{6,54},{7,55},{8,56},{9,... | collective-permute-start | bytes 147464 | tf_op jit(solution)/shard_map/gain16/ppermute | solution.py:434
  210.3 6.1 %attend128.1 = bf16[128,4096]{1,0:T(8,128)(2,1)} custom-call(bf16[256,4096]{1,0:T(8,128)(2,1)S(1)} %get-tuple-element.66.own_ref.other_ref, bf16[256,4096]{1,0:T(8,128)(2,1)S(1)} %get-tuple-element.66.own_ref.other_ref, f32[2,128]{1,0:T(2,128)S(1)} %rsqrt_bitcast_fusion.inverse_ref, f32[3,4096]{1,0:T(4,128)S(1)} %bitcast.60, f32[1,32]{1,0:T(1,128)S(1)} %copy-done.9, ...), custom_call_target="tpu_custom_call" | custom-call | tf_op jit(solution)/shard_map/attend128/pallas_call | solution.py:96
  (99 shorter events, 29.8 us)
Async XLA Ops:
  2.6 53.8 %collective-permute-start.2 = (bf16[128,2048]{1,0:T(8,128)(2,1)}, bf16[128,2048]{1,0:T(8,128)(2,1)}, u32[]{:S(2)}, u32[]{:S(2)}) collective-permute-start(bf16[128,2048]{1,0:T(8,128)(2,1)} %dynamic-slice_bitcast_fusion.1), channel_id=1, source_target_pairs={{0,1},{1,0},{2,3},{3,2},{4,5},{5,4},{6,7},{7,6},{8,9},{9,8},{10,11... | collective-permute-start | bytes 1572872 | tf_op jit(solution)/shard_map/cot_a/ppermute | solution.py:326
  7.8 44.2 %collective-permute-start = (bf16[128,2176]{1,0:T(8,128)(2,1)S(1)}, bf16[128,2176]{1,0:T(8,128)(2,1)S(1)}, u32[]{:S(2)}, u32[]{:S(2)}) collective-permute-start(bf16[128,2176]{1,0:T(8,128)(2,1)S(1)} %fusion.2.inverse_own_ref), channel_id=1, source_target_pairs={{0,1},{1,0},{2,3},{3,2},{4,5},{5,4},{6,7},{7,6},{8,9},{9,8},{10,11... | collective-permute-start | bytes 1671176 | tf_op jit(solution)/shard_map/saved_a/ppermute | solution.py:326
  11.8 44.7 %copy-start.5 = (f32[256,256]{1,0:T(8,128)}, f32[256,256]{1,0:T(8,128)S(1)}, u32[]{:S(2)}) copy-start(f32[256,256]{1,0:T(8,128)S(1)} %get-tuple-element.74.table_ref) | copy-start | bytes 786436
  11.8 44.7 %copy-start.2 = (bf16[1,128,4096]{2,1,0:T(8,128)(2,1)S(1)}, bf16[1,128,4096]{2,1,0:T(8,128)(2,1)}, u32[]{:S(2)}) copy-start(bf16[1,128,4096]{2,1,0:T(8,128)(2,1)} %param.13) | copy-start | bytes 3145732
  11.8 44.7 %copy-start.9 = (f32[1,32]{1,0:T(1,128)S(1)}, f32[1,32]{1,0:T(1,128)}, u32[]{:S(2)}) copy-start(f32[1,32]{1,0:T(1,128)} %slopes_ref.7) | copy-start | bytes 388
  52.0 46.4 %collective-permute-start.1 = (bf16[128,4096]{1,0:T(8,128)(2,1)}, bf16[128,4096]{1,0:T(8,128)(2,1)}, u32[]{:S(2)}, u32[]{:S(2)}) collective-permute-start(bf16[128,4096]{1,0:T(8,128)(2,1)} %bitcast.own_ref), channel_id=1, source_target_pairs={{0,1},{1,0},{2,3},{3,2},{4,5},{5,4},{6,7},{7,6},{8,9},{9,8},{10,11... | collective-permute-start | bytes 3145736 | tf_op jit(solution)/shard_map/acts/ppermute | solution.py:326
  67.0 31.3 %collective-permute-start.3 = (f32[4,2048]{1,0:T(4,128)S(1)}, f32[4,2048]{1,0:T(4,128)S(1)}, u32[]{:S(2)}, u32[]{:S(2)}) collective-permute-start(f32[4,2048]{1,0:T(4,128)S(1)} %get-tuple-element.33.small_ref), channel_id=1, source_target_pairs={{0,1},{1,0},{2,3},{3,2},{4,5},{5,4},{6,7},{7,6},{8,9},{9,8},{10,11... | collective-permute-start | bytes 98312 | tf_op jit(solution)/shard_map/small_a/ppermute | solution.py:326
  105.2 58.8 %collective-permute-start.7 = (bf16[256,2048]{1,0:T(8,128)(2,1)}, bf16[256,2048]{1,0:T(8,128)(2,1)}, u32[]{:S(2)}, u32[]{:S(2)}) collective-permute-start(bf16[256,2048]{1,0:T(8,128)(2,1)} %get-tuple-element.35), channel_id=1, source_target_pairs={{64,0},{128,64},{192,128},{65,1},{129,65},{193,129},{66,2},{130,66... | collective-permute-start | bytes 3145736 | tf_op jit(solution)/shard_map/to_previous/ppermute | solution.py:335
  109.8 48.3 %collective-permute-start.6 = (bf16[128,3072]{1,0:T(8,128)(2,1)}, bf16[128,3072]{1,0:T(8,128)(2,1)}, u32[]{:S(2)}, u32[]{:S(2)}) collective-permute-start(bf16[128,3072]{1,0:T(8,128)(2,1)} %maximum_select_fusion.4), channel_id=1, source_target_pairs={{128,129},{129,128},{130,131},{131,130},{132,133},{133,132},{134,1... | collective-permute-start | bytes 2359304 | tf_op jit(solution)/shard_map/extra/ppermute | solution.py:331
  114.1 40.5 %collective-permute-start.4 = (bf16[128,2176]{1,0:T(8,128)(2,1)S(1)}, bf16[128,2176]{1,0:T(8,128)(2,1)S(1)}, u32[]{:S(2)}, u32[]{:S(2)}) collective-permute-start(bf16[128,2176]{1,0:T(8,128)(2,1)S(1)} %fusion.3.inverse_own_ref), channel_id=1, source_target_pairs={{0,1},{1,0},{2,3},{3,2},{4,5},{5,4},{6,7},{7,6},{8,9},{9,8},{10,11... | collective-permute-start | bytes 1671176 | tf_op jit(solution)/shard_map/saved_b/ppermute | solution.py:326
  116.2 47.8 %copy-start.13 = (bf16[128,2048]{1,0:T(8,128)(2,1)S(1)}, bf16[128,2048]{1,0:T(8,128)(2,1)}, u32[]{:S(2)}) copy-start(bf16[128,2048]{1,0:T(8,128)(2,1)} %get-tuple-element.67) | copy-start | bytes 1572868
  124.6 72.9 %collective-permute-start.11 = (bf16[256,4096]{1,0:T(8,128)(2,1)S(1)}, bf16[256,4096]{1,0:T(8,128)(2,1)S(1)}, u32[]{:S(2)}, u32[]{:S(2)}) collective-permute-start(bf16[256,4096]{1,0:T(8,128)(2,1)S(1)} %get-tuple-element.51), channel_id=1, source_target_pairs={{0,64},{64,128},{128,192},{1,65},{65,129},{129,193},{2,66},{66,130... | collective-permute-start | bytes 6291464 | tf_op jit(solution)/shard_map/to_next/ppermute | solution.py:335
  154.6 27.4 %collective-permute-start.5 = (bf16[128,2048]{1,0:T(8,128)(2,1)}, bf16[128,2048]{1,0:T(8,128)(2,1)S(1)}, u32[]{:S(2)}, u32[]{:S(2)}) collective-permute-start(bf16[128,2048]{1,0:T(8,128)(2,1)} %get-tuple-element.41), channel_id=1, source_target_pairs={{0,1},{1,0},{2,3},{3,2},{4,5},{5,4},{6,7},{7,6},{8,9},{9,8},{10,11... | collective-permute-start | bytes 1572872 | tf_op jit(solution)/shard_map/grad_one/ppermute | solution.py:326
  159.0 19.6 %collective-permute-start.10 = (bf16[128,1024]{1,0:T(8,128)(2,1)S(1)}, bf16[128,1024]{1,0:T(8,128)(2,1)S(1)}, u32[]{:S(2)}, u32[]{:S(2)}) collective-permute-start(bf16[128,1024]{1,0:T(8,128)(2,1)S(1)} %slice.45), channel_id=1, source_target_pairs={{192,0},{193,1},{194,2},{195,3},{196,4},{197,5},{198,6},{199,7},{2... | collective-permute-start | bytes 786440 | tf_op jit(solution)/shard_map/helped/ppermute | solution.py:394
  160.9 24.5 %collective-permute-start.9 = (bf16[128,3072]{1,0:T(8,128)(2,1)}, bf16[128,3072]{1,0:T(8,128)(2,1)S(1)}, u32[]{:S(2)}, u32[]{:S(2)}) collective-permute-start(bf16[128,3072]{1,0:T(8,128)(2,1)} %collective-permute-done.6), channel_id=1, source_target_pairs={{128,0},{129,1},{130,2},{131,3},{132,4},{133,5},{134,6},{135,7},{1... | collective-permute-start | bytes 2359304 | tf_op jit(solution)/shard_map/helped/ppermute | solution.py:393
  174.5 7.9 %collective-permute-start.8 = (f32[4,2048]{1,0:T(4,128)S(1)}, f32[4,2048]{1,0:T(4,128)S(1)}, u32[]{:S(2)}, u32[]{:S(2)}) collective-permute-start(f32[4,2048]{1,0:T(4,128)S(1)} %select_add_fusion.small_ref), channel_id=1, source_target_pairs={{0,1},{1,0},{2,3},{3,2},{4,5},{5,4},{6,7},{7,6},{8,9},{9,8},{10,11... | collective-permute-start | bytes 98312 | tf_op jit(solution)/shard_map/small_b/ppermute | solution.py:326
  185.4 12.0 %collective-permute-start.13 = (f32[3,4096]{1,0:T(4,128)S(1)}, f32[3,4096]{1,0:T(4,128)S(1)}, u32[]{:S(2)}, u32[]{:S(2)}) collective-permute-start(f32[3,4096]{1,0:T(4,128)S(1)} %maximum_select_fusion.5), channel_id=1, source_target_pairs={{0,2},{1,3},{2,0},{3,1},{4,6},{5,7},{6,4},{7,5},{8,10},{9,11},{10,... | collective-permute-start | bytes 147464 | tf_op jit(solution)/shard_map/gain2/ppermute | solution.py:428
  196.1 21.1 %collective-permute-start.12 = (bf16[128,2048]{1,0:T(8,128)(2,1)S(1)}, bf16[128,2048]{1,0:T(8,128)(2,1)S(1)}, u32[]{:S(2)}, u32[]{:S(2)}) collective-permute-start(bf16[128,2048]{1,0:T(8,128)(2,1)S(1)} %get-tuple-element.48), channel_id=1, source_target_pairs={{0,1},{1,0},{2,3},{3,2},{4,5},{5,4},{6,7},{7,6},{8,9},{9,8},{10,11... | collective-permute-start | bytes 1572872 | tf_op jit(solution)/shard_map/bwd_two/ppermute | solution.py:326
  197.5 5.6 %collective-permute-start.16 = (f32[3,4096]{1,0:T(4,128)S(1)}, f32[3,4096]{1,0:T(4,128)S(1)}, u32[]{:S(2)}, u32[]{:S(2)}) collective-permute-start(f32[3,4096]{1,0:T(4,128)S(1)} %add.138), channel_id=1, source_target_pairs={{0,12},{1,13},{2,14},{3,15},{4,8},{5,9},{6,10},{7,11},{8,4},{9,5},... | collective-permute-start | bytes 147464 | tf_op jit(solution)/shard_map/gain4/ppermute | solution.py:434
  200.3 5.8 %collective-permute-start.15 = (f32[3,4096]{1,0:T(4,128)S(1)}, f32[3,4096]{1,0:T(4,128)S(1)}, u32[]{:S(2)}, u32[]{:S(2)}) collective-permute-start(f32[3,4096]{1,0:T(4,128)S(1)} %add.138), channel_id=1, source_target_pairs={{0,8},{1,9},{2,10},{3,11},{4,12},{5,13},{6,14},{7,15},{8,0},{9,1},... | collective-permute-start | bytes 147464 | tf_op jit(solution)/shard_map/gain4/ppermute | solution.py:434
  201.1 5.0 %collective-permute-start.14 = (f32[3,4096]{1,0:T(4,128)S(1)}, f32[3,4096]{1,0:T(4,128)S(1)}, u32[]{:S(2)}, u32[]{:S(2)}) collective-permute-start(f32[3,4096]{1,0:T(4,128)S(1)} %add.138), channel_id=1, source_target_pairs={{0,4},{1,5},{2,6},{3,7},{4,0},{5,1},{6,2},{7,3},{8,12},{9,13},{10,... | collective-permute-start | bytes 147464 | tf_op jit(solution)/shard_map/gain4/ppermute | solution.py:434
  206.1 10.3 %collective-permute-start.19 = (f32[3,4096]{1,0:T(4,128)S(1)}, f32[3,4096]{1,0:T(4,128)S(1)}, u32[]{:S(2)}, u32[]{:S(2)}) collective-permute-start(f32[3,4096]{1,0:T(4,128)S(1)} %add_add_fusion.1), channel_id=1, source_target_pairs={{0,48},{1,49},{2,50},{3,51},{4,52},{5,53},{6,54},{7,55},{8,56},{9,... | collective-permute-start | bytes 147464 | tf_op jit(solution)/shard_map/gain16/ppermute | solution.py:434
  209.2 7.2 %collective-permute-start.18 = (f32[3,4096]{1,0:T(4,128)S(1)}, f32[3,4096]{1,0:T(4,128)S(1)}, u32[]{:S(2)}, u32[]{:S(2)}) collective-permute-start(f32[3,4096]{1,0:T(4,128)S(1)} %add_add_fusion.1), channel_id=1, source_target_pairs={{0,32},{1,33},{2,34},{3,35},{4,36},{5,37},{6,38},{7,39},{8,40},{9,... | collective-permute-start | bytes 147464 | tf_op jit(solution)/shard_map/gain16/ppermute | solution.py:434
  209.9 6.6 %collective-permute-start.17 = (f32[3,4096]{1,0:T(4,128)S(1)}, f32[3,4096]{1,0:T(4,128)S(1)}, u32[]{:S(2)}, u32[]{:S(2)}) collective-permute-start(f32[3,4096]{1,0:T(4,128)S(1)} %add_add_fusion.1), channel_id=1, source_target_pairs={{0,16},{1,17},{2,18},{3,19},{4,20},{5,21},{6,22},{7,23},{8,24},{9,... | collective-permute-start | bytes 147464 | tf_op jit(solution)/shard_map/gain16/ppermute | solution.py:434
  (12 other events, 143.1 us)

commit v3 on v2

--- a/solution.py
+++ b/solution.py
@@ -177,7 +177,7 @@
         grad_key = dot(grad_scores, query, 1, 0)
         grad_query = dot(grad_scores, key, 0, 0)
         grad = grad_query * gains[0:1] + grad_key * gains[1:2] + grad_value * gains[2:3]
-        grad_ref[:, cols] = grad
+        grad_ref[:, cols] = grad.astype(jnp.bfloat16)
         total_ref[...] += grad * wide
         small_ref[0:1, pl.ds((step * heads + head) * HD, HD)] = jnp.sum(grad_query * normed_in, axis=0, keepdims=True)
         small_ref[1:2, pl.ds((step * heads + head) * HD, HD)] = jnp.sum(grad_key * normed_in, axis=0, keepdims=True)
@@ -215,7 +215,7 @@
             scratch_shapes=[pltpu.VMEM((REGION, HD), jnp.float32)] * 2,
         ),
         out_shape=[
-            jax.ShapeDtypeStruct((REGION, HALF), jnp.float32),
+            jax.ShapeDtypeStruct((REGION, HALF), jnp.bfloat16),
             jax.ShapeDtypeStruct((4, HALF), jnp.float32),
         ],
         compiler_params=pltpu.CompilerParams(vmem_limit_bytes=VMEM_LIMIT),
@@ -255,7 +255,7 @@
         for piece in range(out_ref.shape[1] // HD):
             cols = pl.ds(piece * HD, HD)
             wide = hidden[:, cols].astype(jnp.float32) * scale
-            grad = (grad_ref[rows, cols] - wide * mean) * scale
+            grad = (grad_ref[rows, cols].astype(jnp.float32) - wide * mean) * scale
             result = (cot[:, cols].astype(jnp.float32) + grad).astype(jnp.bfloat16)
             out_ref[rows, cols] = result
             if part == 1:
@@ -364,69 +364,57 @@
     is_first = section_index == 0
     is_last = section_index == sections - 1
 
+    with jax.named_scope("acts"):
+        acts_other = swap(acts)
+    saved_a_sent = with_inverse(for_partner(saved_a), inverse_norm(saved_a))
+    saved_b_sent = with_inverse(for_partner(saved_b), inverse_norm(saved_b))
     with jax.named_scope("cot_a"):
-        cot_a_send = for_partner(cot_a)
-        cot_a_other = swap(cot_a_send)
+        cot_a_other = swap(after(for_partner(cot_a), acts_other))
     with jax.named_scope("saved_a"):
-        early = after(saved_a, cot_a_send)
-        saved_a_sent = with_inverse(for_partner(early), inverse_norm(early))
-        saved_a_other = swap(saved_a_sent)
-    saved_b_sent = with_inverse(for_partner(saved_b), inverse_norm(after(saved_b, saved_a_sent)))
-    with jax.named_scope("acts"):
-        acts_other = swap(after(acts, saved_a_other))
-
-    back = (side_vec, saved_a, saved_a_sent, saved_a_other, cot_a, cot_a_other)
-    grad, small_a = backward(*back, gain_rows, slopes, by_key, keep)
-    with jax.named_scope("small_a"):
-        received_a = swap(small_a)
-    received_a = after(received_a, acts_other)
-    first, first_other = combine(*back, grad, small_a, received_a)
-    with jax.named_scope("to_previous"):
-        from_next = shifted(first, -1)
-    with jax.named_scope("saved_b"):
-        saved_b_other = swap(after(saved_b_sent, acts_other))
-    with jax.named_scope("extra"):
-        extra = jnp.concatenate([first_in[:, LATE:], for_partner(cot_last)], axis=1)
-        extra = jnp.where(is_last, extra, first_in[:, :LATE])
-        received_extra = swap_in((sections - 2, sections - 1), after(extra, acts_other))
-    with jax.named_scope("helped"):
-        early_part = lax.ppermute(received_extra, "section", [(sections - 2, 0)])
-        late_part = lax.ppermute(received_extra[:, : D - LATE], "section", [(sections - 1, 0)])
-
-    acts_other = after(acts_other, first)
+        saved_a_other = swap(after(saved_a_sent, acts_other))
     inverse = jnp.stack([inverse_norm(acts), inverse_norm(acts_other)])
     out_one, out_region = forward(
         REGION, acts, acts_other, inverse, gain_rows, slopes, by_query, keep
     )
     with jax.named_scope("to_next"):
         from_before = shifted(out_region, 1)
+
+    back = (side_vec, saved_a, saved_a_sent, after(saved_a_other, out_one), cot_a, cot_a_other)
+    grad, small_a = backward(*back, gain_rows, slopes, by_key, keep)
+    with jax.named_scope("small_a"):
+        received_a = swap(small_a)
+    with jax.named_scope("saved_b"):
+        saved_b_other = swap(after(saved_b_sent, saved_a_other, out_one))
+    with jax.named_scope("cot_last"):
+        cot_last_send = after(for_partner(cot_last), saved_a_other, out_one)
+        cot_last_other = swap_in((sections - 1,), cot_last_send)
+    received_a = after(received_a, saved_b_other, cot_last_other)
+    first, first_other = combine(*back, grad, small_a, received_a)
+    with jax.named_scope("to_previous"):
+        from_next = shifted(first, -1)
     with jax.named_scope("grad_one"):
-        grad_one_part = swap(after(first_other, saved_b_other))
-
-    cot_b = jnp.concatenate([for_me(cot_last), received_extra[:, D - LATE :]], axis=0)
-    cot_b = after(jnp.where(is_last, cot_b, from_next), out_one)
+        grad_one_part = swap(first_other)
+
+    cot_b = jnp.concatenate([for_me(cot_last), cot_last_other], axis=0)
+    cot_b = after(jnp.where(is_last, cot_b, from_next), from_before)
+    with jax.named_scope("first_in"):
+        first_in_other = swap_in((0,), after(first_in, from_next))
     back = (side_vec, saved_b, saved_b_sent, saved_b_other, cot_b, cot_b)
     grad, small_b = backward(*back, gain_rows, slopes, by_key, keep)
     small = small_b + jnp.where(jnp.arange(4)[:, None] < 3, small_a, 0.0)
     with jax.named_scope("small_b"):
         received_b = swap(small)
-    received_b = after(received_b, grad_one_part, early_part, late_part)
-    gain_total = joined(small[:3], received_b[:3])
-    received_b = after(received_b, gain_total)
+    received_b = after(received_b, grad_one_part, first_in_other)
     second, second_other = combine(*back, grad, small, received_b)
     with jax.named_scope("bwd_two"):
         bwd_two_part = swap(second_other)
 
-    fed = jnp.concatenate([after(early_part, second_other), late_part], axis=1)
-    fed = jnp.concatenate([first_in, fed], axis=0)
+    fed = jnp.concatenate([first_in, after(first_in_other, second_other)], axis=0)
     region_in = jnp.where(is_first, fed, from_before)
     inverse = inverse_norm(region_in).reshape(2, OWN)
     (fwd_two,) = forward(OWN, region_in, region_in, inverse, gain_rows, slopes, by_query, keep)
 
-    if devices > 2:
-        with jax.named_scope("gain2"):
-            gain_total = gain_total + lax.ppermute(gain_total, "seq", flips(2))
-    gain_total = after(gain_total, from_before)
+    gain_total = joined(small[:3], after(received_b, second_other)[:3])
     for bit in (4, 16):
         if bit < devices:
             with jax.named_scope("gain" + str(bit)):
@@ -434,6 +422,9 @@
                     lax.ppermute(gain_total, "seq", flips(bit * flip)) for flip in range(1, 4)
                 ]
             gain_total = (gain_total + terms[0]) + (terms[1] + terms[2])
+    if devices > 2:
+        with jax.named_scope("gain2"):
+            gain_total = gain_total + lax.ppermute(gain_total, "seq", flips(2))
 
     bwd_two_part = after(bwd_two_part, fwd_two, gain_total)
 

time: 223 us -> 213 us (0.955); the launches traced: 218 us -> 212 us
  waiting for transfers between devices: 107 us -> 81.5 us
  starting transfers between devices: 45.1 us -> 67 us
  local copies, waits for them, and re-layouts: 15.1 us -> 11 us
  other arithmetic: 12.3 us -> 15.2 us
    ppermute x8, waiting for transfers between devices: 100 us -> 55 us  [swap(): return lax.ppermute(value, 'seq', flips(1))]
    ppermute x8, starting transfers between devices: 13.9 us -> 41.3 us  [swap(): return lax.ppermute(value, 'seq', flips(1))]
    ppermute x2, waiting for transfers between devices: 0.01 us -> 19.5 us  [shifted(): lax.ppermute(value, 'section', [(s, s + steps) for s in range(first, last)])]
    ppermute x1, waiting for transfers between devices: 0.01 us -> 4.32 us  [on_device(): gain_total = gain_total + lax.ppermute(gain_total, 'seq', flips(2))]
    ppermute x2 -> x0, starting transfers between devices: 3.91 us -> none  [the longest x1 3.1 us: on_device(): early_part = lax.ppermute(received_extra, 'section', [(sections - 2, 0)])]
    ppermute x2 -> x0, waiting for transfers between devices: 2.97 us -> none  [the longest x1 2.97 us: on_device(): early_part = lax.ppermute(received_extra, 'section', [(sections - 2, 0)])]
    ppermute x1 -> x2, starting transfers between devices: 4.3 us -> 1.4 us  [swap_in(): return lax.ppermute(value, ('section', 'seq'), pairs)]
    unnamed x32 -> x42, local copies, waits for them, and re-layouts: 4.92 us -> 4.55 us
  transfers between devices with their start and end apart: 20 -> 19, of which waited for: 8 -> 10; matrix products, arithmetic and copies ran while one was open for 9% -> 10% of each run, Pallas kernels for 16% -> 16%
where the time goes in v3:
time: 213 us; the launch traced here: 212 us
  waiting for transfers between devices  81.5 us (38%)
  starting transfers between devices  67 us (31%)
  Pallas kernels  36.3 us (17%)
  other arithmetic  15.2 us (7%)
  local copies, waits for them, and re-layouts  11 us (5%)
    ppermute x8, waiting for transfers between devices, swap(): return lax.ppermute(value, 'seq', flips(1))  55 us
    ppermute x8, starting transfers between devices, swap(): return lax.ppermute(value, 'seq', flips(1))  41.3 us
    ppermute x2, waiting for transfers between devices, shifted(): lax.ppermute(value, 'section', [(s, s + steps) for s in range(first, last)])  19.5 us
    pallas_call x2, Pallas kernels, backward(): pl.pallas_call(functools.partial(backward_body, STEP_HEADS), grid_spec=pl...  17.5 us
    pallas_call x2, Pallas kernels, forward(): pl.pallas_call(functools.partial(forward_body, query_rows, STEP_HEADS), g...  14.7 us
    ppermute x1, starting transfers between devices, on_device(): gain_total = gain_total + lax.ppermute(gain_total, 'seq', flips(2))  9.23 us
    ppermute x6, starting transfers between devices, on_device(): lax.ppermute(gain_total, 'seq', flips(bit * flip))  8.67 us
    reduce_sum x5, other arithmetic, inverse_norm(): return lax.rsqrt(jnp.mean(wide * wide, axis=1) + 1e-05)  7.58 us
  transfers between devices with their start and end apart: 19, of which 10 were waited for; matrix products, arithmetic and copies ran while one was open for 10% of the time, Pallas kernels for 16%

profile of v3, /device:TPU:32, one launch (start us, length us, event | category | flops | bytes accessed | tf_op | source)
XLA Modules:
  0.0 212.0 jit_solution(9772033160034955407)
XLA Ops:
  0.7 3.4 %collective-permute-start = (bf16[128,4096]{1,0:T(8,128)(2,1)}, bf16[128,4096]{1,0:T(8,128)(2,1)}, u32[]{:S(2)}, u32[]{:S(2)}) collective-permute-start(bf16[128,4096]{1,0:T(8,128)(2,1)} %bitcast.58), channel_id=1, source_target_pairs={{0,1},{1,0},{2,3},{3,2},{4,5},{5,4},{6,7},{7,6},{8,9},{9,8},{10,11... | collective-permute-start | bytes 3145736 | tf_op jit(solution)/shard_map/acts/ppermute | solution.py:326
  14.9 33.9 %collective-permute-done.other_ref = bf16[128,4096]{1,0:T(8,128)(2,1)} collective-permute-done((bf16[128,4096]{1,0:T(8,128)(2,1)}, bf16[128,4096]{1,0:T(8,128)(2,1)}, u32[]{:S(2)}, u32[]{:S(2)}) %collective-permute-start) | collective-permute-done | bytes 1048608 | tf_op jit(solution)/shard_map/acts/ppermute | solution.py:326
  48.8 26.5 %collective-permute-start.1 = (bf16[128,2176]{1,0:T(8,128)(2,1)S(1)}, bf16[128,2176]{1,0:T(8,128)(2,1)S(1)}, u32[]{:S(2)}, u32[]{:S(2)}) collective-permute-start(bf16[128,2176]{1,0:T(8,128)(2,1)S(1)} %fusion.2.inverse_own_ref), channel_id=1, source_target_pairs={{0,1},{1,0},{2,3},{3,2},{4,5},{5,4},{6,7},{7,6},{8,9},{9,8},{10,11... | collective-permute-start | bytes 1671176 | tf_op jit(solution)/shard_map/saved_a/ppermute | solution.py:326
  79.4 8.6 %attend256.1 = (bf16[128,4096]{1,0:T(8,128)(2,1)}, bf16[256,4096]{1,0:T(8,128)(2,1)}) custom-call(bf16[128,4096]{1,0:T(8,128)(2,1)S(1)} %bitcast.59, bf16[128,4096]{1,0:T(8,128)(2,1)} %collective-permute-done.other_ref, f32[2,128]{1,0:T(2,128)S(1)} %pad_maximum_fusion.inverse_ref, f32[3,4096]{1,0:T(4,128)S(1)} %bitcast.60, f32[1,32]{1,0:T(1,128)S(1)} %copy-done.13, ...), custom_call_target="tpu_custom_call" | custom-call | tf_op jit(solution)/shard_map/attend256/pallas_call | solution.py:96
  88.1 2.0 collective-permute-start.8
  90.1 4.3 %collective-permute-done.1.other_ref.inverse_other_ref = bf16[128,2176]{1,0:T(8,128)(2,1)S(1)} collective-permute-done((bf16[128,2176]{1,0:T(8,128)(2,1)S(1)}, bf16[128,2176]{1,0:T(8,128)(2,1)S(1)}, u32[]{:S(2)}, u32[]{:S(2)}) %collective-permute-start.1) | collective-permute-done | bytes 557088 | tf_op jit(solution)/shard_map/saved_a/ppermute | solution.py:326
  94.4 3.5 %collective-permute-start.4 = (bf16[128,2176]{1,0:T(8,128)(2,1)S(1)}, bf16[128,2176]{1,0:T(8,128)(2,1)S(1)}, u32[]{:S(2)}, u32[]{:S(2)}) collective-permute-start(bf16[128,2176]{1,0:T(8,128)(2,1)S(1)} %copy-done.4), channel_id=1, source_target_pairs={{0,1},{1,0},{2,3},{3,2},{4,5},{5,4},{6,7},{7,6},{8,9},{9,8},{10,11... | collective-permute-start | bytes 1671176 | tf_op jit(solution)/shard_map/saved_b/ppermute | solution.py:326
  99.4 6.3 %collective-permute-done.2.cot_other_ref = bf16[128,2048]{1,0:T(8,128)(2,1)S(1)} collective-permute-done((bf16[128,2048]{1,0:T(8,128)(2,1)}, bf16[128,2048]{1,0:T(8,128)(2,1)S(1)}, u32[]{:S(2)}, u32[]{:S(2)}) %collective-permute-start.2) | collective-permute-done | bytes 524320 | tf_op jit(solution)/shard_map/cot_a/ppermute | solution.py:326
  105.8 8.8 %differentiate.2 = (bf16[256,2048]{1,0:T(8,128)(2,1)S(1)}, f32[4,2048]{1,0:T(4,128)S(1)}) custom-call(s32[1]{0:T(128)} %bitcast.8.side_ref, bf16[128,4096]{1,0:T(8,128)(2,1)S(1)} %bitcast.52, bf16[128,2176]{1,0:T(8,128)(2,1)S(1)} %collective-permute-done.1.other_ref.inverse_other_ref, bf16[128,4096]{1,0:T(8,128)(2,1)S(1)} %bitcast.56, ...), custom_call_target="tpu_custom_call" | custom-call | tf_op jit(solution)/shard_map/differentiate/pallas_call | solution.py:201
  114.5 3.4 %collective-permute-start.3 = (f32[4,2048]{1,0:T(4,128)S(1)}, f32[4,2048]{1,0:T(4,128)S(1)}, u32[]{:S(2)}, u32[]{:S(2)}) collective-permute-start(f32[4,2048]{1,0:T(4,128)S(1)} %get-tuple-element.33.small_ref), channel_id=1, source_target_pairs={{0,1},{1,0},{2,3},{3,2},{4,5},{5,4},{6,7},{7,6},{8,9},{9,8},{10,11... | collective-permute-start | bytes 98312 | tf_op jit(solution)/shard_map/small_a/ppermute | solution.py:326
  118.0 6.7 %collective-permute-done.3.received_ref = f32[4,2048]{1,0:T(4,128)S(1)} collective-permute-done((f32[4,2048]{1,0:T(4,128)S(1)}, f32[4,2048]{1,0:T(4,128)S(1)}, u32[]{:S(2)}, u32[]{:S(2)}) %collective-permute-start.3) | collective-permute-done | bytes 32800 | tf_op jit(solution)/shard_map/small_a/ppermute | solution.py:326
  125.5 2.5 %combine.2 = (bf16[256,2048]{1,0:T(8,128)(2,1)}, bf16[128,2048]{1,0:T(8,128)(2,1)S(1)}) custom-call(s32[1]{0:T(128)} %bitcast.8.side_ref, bf16[128,4096]{1,0:T(8,128)(2,1)S(1)} %bitcast.53, bf16[128,2176]{1,0:T(8,128)(2,1)S(1)} %collective-permute-done.1.other_ref.inverse_other_ref, bf16[128,4096]{1,0:T(8,128)(2,1)S(1)} %bitcast.57, ...), custom_call_target="tpu_custom_call" | custom-call | tf_op jit(solution)/shard_map/combine/pallas_call | solution.py:268
  128.8 4.3 %collective-permute-start.7 = (bf16[256,2048]{1,0:T(8,128)(2,1)}, bf16[256,2048]{1,0:T(8,128)(2,1)}, u32[]{:S(2)}, u32[]{:S(2)}) collective-permute-start(bf16[256,2048]{1,0:T(8,128)(2,1)} %get-tuple-element.37), channel_id=1, source_target_pairs={{64,0},{128,64},{192,128},{65,1},{129,65},{193,129},{66,2},{130,66... | collective-permute-start | bytes 3145736 | tf_op jit(solution)/shard_map/to_previous/ppermute | solution.py:335
  134.4 19.5 %collective-permute-done.7 = bf16[256,2048]{1,0:T(8,128)(2,1)} collective-permute-done((bf16[256,2048]{1,0:T(8,128)(2,1)}, bf16[256,2048]{1,0:T(8,128)(2,1)}, u32[]{:S(2)}, u32[]{:S(2)}) %collective-permute-start.7) | collective-permute-done | bytes 1048608 | tf_op jit(solution)/shard_map/to_previous/ppermute | solution.py:335
  156.6 8.7 %differentiate.3 = (bf16[256,2048]{1,0:T(8,128)(2,1)S(1)}, f32[4,2048]{1,0:T(4,128)S(1)}) custom-call(s32[1]{0:T(128)} %bitcast.8.side_ref, bf16[128,4096]{1,0:T(8,128)(2,1)S(1)} %bitcast.54, bf16[128,2176]{1,0:T(8,128)(2,1)S(1)} %collective-permute-done.4.other_ref.inverse_other_ref, bf16[256,2048]{1,0:T(8,128)(2,1)S(1)} %maximum_select_fusion.1.cot_own_ref.cot_other_ref, ...), custom_call_target="tpu_custom_call" | custom-call | tf_op jit(solution)/shard_map/differentiate/pallas_call | solution.py:201
  166.7 3.2 %collective-permute-done.6 = bf16[128,2048]{1,0:T(8,128)(2,1)S(1)} collective-permute-done((bf16[128,2048]{1,0:T(8,128)(2,1)}, bf16[128,2048]{1,0:T(8,128)(2,1)S(1)}, u32[]{:S(2)}, u32[]{:S(2)}) %collective-permute-start.6) | collective-permute-done | bytes 524320 | tf_op jit(solution)/shard_map/grad_one/ppermute | solution.py:326
  172.1 3.5 %collective-permute-start.14 = (f32[3,4096]{1,0:T(4,128)S(1)}, f32[3,4096]{1,0:T(4,128)S(1)}, u32[]{:S(2)}, u32[]{:S(2)}) collective-permute-start(f32[3,4096]{1,0:T(4,128)S(1)} %maximum_select_fusion.4), channel_id=1, source_target_pairs={{0,12},{1,13},{2,14},{3,15},{4,8},{5,9},{6,10},{7,11},{8,4},{9,5},... | collective-permute-start | bytes 147464 | tf_op jit(solution)/shard_map/gain4/ppermute | solution.py:422
  176.6 3.0 %collective-permute-start.11 = (bf16[128,2048]{1,0:T(8,128)(2,1)S(1)}, bf16[128,2048]{1,0:T(8,128)(2,1)S(1)}, u32[]{:S(2)}, u32[]{:S(2)}) collective-permute-start(bf16[128,2048]{1,0:T(8,128)(2,1)S(1)} %get-tuple-element.45), channel_id=1, source_target_pairs={{0,1},{1,0},{2,3},{3,2},{4,5},{5,4},{6,7},{7,6},{8,9},{9,8},{10,11... | collective-permute-start | bytes 1572872 | tf_op jit(solution)/shard_map/bwd_two/ppermute | solution.py:326
  181.5 3.1 %collective-permute-start.17 = (f32[3,4096]{1,0:T(4,128)S(1)}, f32[3,4096]{1,0:T(4,128)S(1)}, u32[]{:S(2)}, u32[]{:S(2)}) collective-permute-start(f32[3,4096]{1,0:T(4,128)S(1)} %add_add_fusion.1), channel_id=1, source_target_pairs={{0,48},{1,49},{2,50},{3,51},{4,52},{5,53},{6,54},{7,55},{8,56},{9,... | collective-permute-start | bytes 147464 | tf_op jit(solution)/shard_map/gain16/ppermute | solution.py:422
  185.6 2.6 %multiply_reduce_fusion = (f32[256]{0:T(256)S(1)}, bf16[256,4096]{1,0:T(8,128)(2,1)S(1)}) fusion(bf16[256,4096]{1,0:T(8,128)(2,1)} %collective-permute-done.8, bf16[128,4096]{1,0:T(8,128)(2,1)S(1)} %collective-permute-done.10, bf16[128,4096]{1,0:T(8,128)(2,1)S(1)} %copy-done.17, pred[]{:T(512)S(6)} %eq.15), kind=kLoop, calls=%fused_computation | loop fusion | flops 8388352 | bytes 6292481 | tf_op jit(solution)/shard_map/reduce_sum | solution.py:307
  188.2 2.1 collective-permute-done.16
  190.4 9.2 %collective-permute-start.18 = (f32[3,4096]{1,0:T(4,128)S(1)}, f32[3,4096]{1,0:T(4,128)S(1)}, u32[]{:S(2)}, u32[]{:S(2)}) collective-permute-start(f32[3,4096]{1,0:T(4,128)S(1)} %add_add_fusion), channel_id=1, source_target_pairs={{0,2},{1,3},{2,0},{3,1},{4,6},{5,7},{6,4},{7,5},{8,10},{9,11},{10,... | collective-permute-start | bytes 147464 | tf_op jit(solution)/shard_map/gain2/ppermute | solution.py:427
  199.6 6.1 %attend128.1 = bf16[128,4096]{1,0:T(8,128)(2,1)} custom-call(bf16[256,4096]{1,0:T(8,128)(2,1)S(1)} %get-tuple-element.62.own_ref.other_ref, bf16[256,4096]{1,0:T(8,128)(2,1)S(1)} %get-tuple-element.62.own_ref.other_ref, f32[2,128]{1,0:T(2,128)S(1)} %rsqrt_bitcast_fusion.inverse_ref, f32[3,4096]{1,0:T(4,128)S(1)} %bitcast.63, f32[1,32]{1,0:T(1,128)S(1)} %copy-done.13, ...), custom_call_target="tpu_custom_call" | custom-call | tf_op jit(solution)/shard_map/attend128/pallas_call | solution.py:96
  205.7 4.3 %collective-permute-done.18 = f32[3,4096]{1,0:T(4,128)S(1)} collective-permute-done((f32[3,4096]{1,0:T(4,128)S(1)}, f32[3,4096]{1,0:T(4,128)S(1)}, u32[]{:S(2)}, u32[]{:S(2)}) %collective-permute-start.18) | collective-permute-done | bytes 49184 | tf_op jit(solution)/shard_map/gain2/ppermute | solution.py:427
  (102 shorter events, 31.4 us)
Async XLA Ops:
  0.7 48.2 %collective-permute-start = (bf16[128,4096]{1,0:T(8,128)(2,1)}, bf16[128,4096]{1,0:T(8,128)(2,1)}, u32[]{:S(2)}, u32[]{:S(2)}) collective-permute-start(bf16[128,4096]{1,0:T(8,128)(2,1)} %bitcast.58), channel_id=1, source_target_pairs={{0,1},{1,0},{2,3},{3,2},{4,5},{5,4},{6,7},{7,6},{8,9},{9,8},{10,11... | collective-permute-start | bytes 3145736 | tf_op jit(solution)/shard_map/acts/ppermute | solution.py:326
  9.2 66.1 %copy-start.19 = (f32[1,3,4096]{2,0,1:T(1,128)S(1)}, f32[1,3,4096]{2,0,1:T(1,128)}, u32[]{:S(2)}) copy-start(f32[1,3,4096]{2,0,1:T(1,128)} %param.16) | copy-start | bytes 147460
  11.9 65.3 %copy-start.13 = (f32[1,32]{1,0:T(1,128)S(1)}, f32[1,32]{1,0:T(1,128)}, u32[]{:S(2)}) copy-start(f32[1,32]{1,0:T(1,128)} %slopes_ref.7) | copy-start | bytes 388
  14.0 74.0 %copy-start.6 = (bf16[128,2176]{1,0:T(8,128)(2,1)}, bf16[128,2176]{1,0:T(8,128)(2,1)S(1)}, u32[]{:S(2)}) copy-start(bf16[128,2176]{1,0:T(8,128)(2,1)S(1)} %fusion.2.inverse_own_ref) | copy-start | bytes 1671172
  48.8 45.6 %collective-permute-start.1 = (bf16[128,2176]{1,0:T(8,128)(2,1)S(1)}, bf16[128,2176]{1,0:T(8,128)(2,1)S(1)}, u32[]{:S(2)}, u32[]{:S(2)}) collective-permute-start(bf16[128,2176]{1,0:T(8,128)(2,1)S(1)} %fusion.2.inverse_own_ref), channel_id=1, source_target_pairs={{0,1},{1,0},{2,3},{3,2},{4,5},{5,4},{6,7},{7,6},{8,9},{9,8},{10,11... | collective-permute-start | bytes 1671176 | tf_op jit(solution)/shard_map/saved_a/ppermute | solution.py:326
  75.5 30.2 %collective-permute-start.2 = (bf16[128,2048]{1,0:T(8,128)(2,1)}, bf16[128,2048]{1,0:T(8,128)(2,1)S(1)}, u32[]{:S(2)}, u32[]{:S(2)}) collective-permute-start(bf16[128,2048]{1,0:T(8,128)(2,1)} %dynamic-slice_bitcast_fusion.1), channel_id=1, source_target_pairs={{0,1},{1,0},{2,3},{3,2},{4,5},{5,4},{6,7},{7,6},{8,9},{9,8},{10,11... | collective-permute-start | bytes 1572872 | tf_op jit(solution)/shard_map/cot_a/ppermute | solution.py:326
  88.1 68.5 %collective-permute-start.8 = (bf16[256,4096]{1,0:T(8,128)(2,1)}, bf16[256,4096]{1,0:T(8,128)(2,1)}, u32[]{:S(2)}, u32[]{:S(2)}) collective-permute-start(bf16[256,4096]{1,0:T(8,128)(2,1)} %get-tuple-element.39), channel_id=1, source_target_pairs={{0,64},{64,128},{128,192},{1,65},{65,129},{129,193},{2,66},{66,130... | collective-permute-start | bytes 6291464 | tf_op jit(solution)/shard_map/to_next/ppermute | solution.py:335
  94.4 30.3 %collective-permute-start.4 = (bf16[128,2176]{1,0:T(8,128)(2,1)S(1)}, bf16[128,2176]{1,0:T(8,128)(2,1)S(1)}, u32[]{:S(2)}, u32[]{:S(2)}) collective-permute-start(bf16[128,2176]{1,0:T(8,128)(2,1)S(1)} %copy-done.4), channel_id=1, source_target_pairs={{0,1},{1,0},{2,3},{3,2},{4,5},{5,4},{6,7},{7,6},{8,9},{9,8},{10,11... | collective-permute-start | bytes 1671176 | tf_op jit(solution)/shard_map/saved_b/ppermute | solution.py:326
  98.7 25.9 %collective-permute-start.5 = (bf16[128,2048]{1,0:T(8,128)(2,1)S(1)}, bf16[128,2048]{1,0:T(8,128)(2,1)S(1)}, u32[]{:S(2)}, u32[]{:S(2)}) collective-permute-start(bf16[128,2048]{1,0:T(8,128)(2,1)S(1)} %get-tuple-element.35), channel_id=1, source_target_pairs={{192,193},{193,192},{194,195},{195,194},{196,197},{197,196},{198,1... | collective-permute-start | bytes 1572872 | tf_op jit(solution)/shard_map/cot_last/ppermute | solution.py:331
  114.5 10.1 %collective-permute-start.3 = (f32[4,2048]{1,0:T(4,128)S(1)}, f32[4,2048]{1,0:T(4,128)S(1)}, u32[]{:S(2)}, u32[]{:S(2)}) collective-permute-start(f32[4,2048]{1,0:T(4,128)S(1)} %get-tuple-element.33.small_ref), channel_id=1, source_target_pairs={{0,1},{1,0},{2,3},{3,2},{4,5},{5,4},{6,7},{7,6},{8,9},{9,8},{10,11... | collective-permute-start | bytes 98312 | tf_op jit(solution)/shard_map/small_a/ppermute | solution.py:326
  128.8 27.8 %copy-start.5 = (bf16[128,2176]{1,0:T(8,128)(2,1)S(1)}, bf16[128,2176]{1,0:T(8,128)(2,1)}, u32[]{:S(2)}) copy-start(bf16[128,2176]{1,0:T(8,128)(2,1)} %fusion.3.inverse_own_ref) | copy-start | bytes 1671172
  128.8 27.8 %copy-start.12 = (f32[256,256]{1,0:T(8,128)S(1)}, f32[256,256]{1,0:T(8,128)}, u32[]{:S(2)}) copy-start(f32[256,256]{1,0:T(8,128)} %get-tuple-element.69.table_ref) | copy-start | bytes 786436
  128.8 25.1 %collective-permute-start.7 = (bf16[256,2048]{1,0:T(8,128)(2,1)}, bf16[256,2048]{1,0:T(8,128)(2,1)}, u32[]{:S(2)}, u32[]{:S(2)}) collective-permute-start(bf16[256,2048]{1,0:T(8,128)(2,1)} %get-tuple-element.37), channel_id=1, source_target_pairs={{64,0},{128,64},{192,128},{65,1},{129,65},{193,129},{66,2},{130,66... | collective-permute-start | bytes 3145736 | tf_op jit(solution)/shard_map/to_previous/ppermute | solution.py:335
  133.2 36.7 %collective-permute-start.6 = (bf16[128,2048]{1,0:T(8,128)(2,1)}, bf16[128,2048]{1,0:T(8,128)(2,1)S(1)}, u32[]{:S(2)}, u32[]{:S(2)}) collective-permute-start(bf16[128,2048]{1,0:T(8,128)(2,1)} %copy-done.14), channel_id=1, source_target_pairs={{0,1},{1,0},{2,3},{3,2},{4,5},{5,4},{6,7},{7,6},{8,9},{9,8},{10,11... | collective-permute-start | bytes 1572872 | tf_op jit(solution)/shard_map/grad_one/ppermute | solution.py:326
  153.9 16.6 %collective-permute-start.10 = (bf16[128,4096]{1,0:T(8,128)(2,1)}, bf16[128,4096]{1,0:T(8,128)(2,1)S(1)}, u32[]{:S(2)}, u32[]{:S(2)}) collective-permute-start(bf16[128,4096]{1,0:T(8,128)(2,1)} %param.11), channel_id=1, source_target_pairs={{0,1},{1,0},{2,3},{3,2},{4,5},{5,4},{6,7},{7,6},{8,9},{9,8},{10,11... | collective-permute-start | bytes 3145736 | tf_op jit(solution)/shard_map/first_in/ppermute | solution.py:331
  165.4 5.1 %collective-permute-start.9 = (f32[4,2048]{1,0:T(4,128)S(1)}, f32[4,2048]{1,0:T(4,128)S(1)}, u32[]{:S(2)}, u32[]{:S(2)}) collective-permute-start(f32[4,2048]{1,0:T(4,128)S(1)} %select_add_fusion.small_ref), channel_id=1, source_target_pairs={{0,1},{1,0},{2,3},{3,2},{4,5},{5,4},{6,7},{7,6},{8,9},{9,8},{10,11... | collective-permute-start | bytes 98312 | tf_op jit(solution)/shard_map/small_b/ppermute | solution.py:326
  172.1 8.8 %collective-permute-start.14 = (f32[3,4096]{1,0:T(4,128)S(1)}, f32[3,4096]{1,0:T(4,128)S(1)}, u32[]{:S(2)}, u32[]{:S(2)}) collective-permute-start(f32[3,4096]{1,0:T(4,128)S(1)} %maximum_select_fusion.4), channel_id=1, source_target_pairs={{0,12},{1,13},{2,14},{3,15},{4,8},{5,9},{6,10},{7,11},{8,4},{9,5},... | collective-permute-start | bytes 147464 | tf_op jit(solution)/shard_map/gain4/ppermute | solution.py:422
  175.6 5.8 %collective-permute-start.13 = (f32[3,4096]{1,0:T(4,128)S(1)}, f32[3,4096]{1,0:T(4,128)S(1)}, u32[]{:S(2)}, u32[]{:S(2)}) collective-permute-start(f32[3,4096]{1,0:T(4,128)S(1)} %maximum_select_fusion.4), channel_id=1, source_target_pairs={{0,8},{1,9},{2,10},{3,11},{4,12},{5,13},{6,14},{7,15},{8,0},{9,1},... | collective-permute-start | bytes 147464 | tf_op jit(solution)/shard_map/gain4/ppermute | solution.py:422
  176.4 5.0 %collective-permute-start.12 = (f32[3,4096]{1,0:T(4,128)S(1)}, f32[3,4096]{1,0:T(4,128)S(1)}, u32[]{:S(2)}, u32[]{:S(2)}) collective-permute-start(f32[3,4096]{1,0:T(4,128)S(1)} %maximum_select_fusion.4), channel_id=1, source_target_pairs={{0,4},{1,5},{2,6},{3,7},{4,0},{5,1},{6,2},{7,3},{8,12},{9,13},{10,... | collective-permute-start | bytes 147464 | tf_op jit(solution)/shard_map/gain4/ppermute | solution.py:422
  176.6 34.1 %collective-permute-start.11 = (bf16[128,2048]{1,0:T(8,128)(2,1)S(1)}, bf16[128,2048]{1,0:T(8,128)(2,1)S(1)}, u32[]{:S(2)}, u32[]{:S(2)}) collective-permute-start(bf16[128,2048]{1,0:T(8,128)(2,1)S(1)} %get-tuple-element.45), channel_id=1, source_target_pairs={{0,1},{1,0},{2,3},{3,2},{4,5},{5,4},{6,7},{7,6},{8,9},{9,8},{10,11... | collective-permute-start | bytes 1572872 | tf_op jit(solution)/shard_map/bwd_two/ppermute | solution.py:326
  181.5 6.8 %collective-permute-start.17 = (f32[3,4096]{1,0:T(4,128)S(1)}, f32[3,4096]{1,0:T(4,128)S(1)}, u32[]{:S(2)}, u32[]{:S(2)}) collective-permute-start(f32[3,4096]{1,0:T(4,128)S(1)} %add_add_fusion.1), channel_id=1, source_target_pairs={{0,48},{1,49},{2,50},{3,51},{4,52},{5,53},{6,54},{7,55},{8,56},{9,... | collective-permute-start | bytes 147464 | tf_op jit(solution)/shard_map/gain16/ppermute | solution.py:422
  184.6 5.8 %collective-permute-start.16 = (f32[3,4096]{1,0:T(4,128)S(1)}, f32[3,4096]{1,0:T(4,128)S(1)}, u32[]{:S(2)}, u32[]{:S(2)}) collective-permute-start(f32[3,4096]{1,0:T(4,128)S(1)} %add_add_fusion.1), channel_id=1, source_target_pairs={{0,32},{1,33},{2,34},{3,35},{4,36},{5,37},{6,38},{7,39},{8,40},{9,... | collective-permute-start | bytes 147464 | tf_op jit(solution)/shard_map/gain16/ppermute | solution.py:422
  185.2 5.1 %collective-permute-start.15 = (f32[3,4096]{1,0:T(4,128)S(1)}, f32[3,4096]{1,0:T(4,128)S(1)}, u32[]{:S(2)}, u32[]{:S(2)}) collective-permute-start(f32[3,4096]{1,0:T(4,128)S(1)} %add_add_fusion.1), channel_id=1, source_target_pairs={{0,16},{1,17},{2,18},{3,19},{4,20},{5,21},{6,22},{7,23},{8,24},{9,... | collective-permute-start | bytes 147464 | tf_op jit(solution)/shard_map/gain16/ppermute | solution.py:422
  190.4 19.7 %collective-permute-start.18 = (f32[3,4096]{1,0:T(4,128)S(1)}, f32[3,4096]{1,0:T(4,128)S(1)}, u32[]{:S(2)}, u32[]{:S(2)}) collective-permute-start(f32[3,4096]{1,0:T(4,128)S(1)} %add_add_fusion), channel_id=1, source_target_pairs={{0,2},{1,3},{2,0},{3,1},{4,6},{5,7},{6,4},{7,5},{8,10},{9,11},{10,... | collective-permute-start | bytes 147464 | tf_op jit(solution)/shard_map/gain2/ppermute | solution.py:427
  (15 other events, 165.0 us)

commit v4 on v3

--- a/solution.py
+++ b/solution.py
@@ -415,16 +415,13 @@
     (fwd_two,) = forward(OWN, region_in, region_in, inverse, gain_rows, slopes, by_query, keep)
 
     gain_total = joined(small[:3], after(received_b, second_other)[:3])
-    for bit in (4, 16):
-        if bit < devices:
-            with jax.named_scope("gain" + str(bit)):
-                terms = [
-                    lax.ppermute(gain_total, "seq", flips(bit * flip)) for flip in range(1, 4)
-                ]
-            gain_total = (gain_total + terms[0]) + (terms[1] + terms[2])
-    if devices > 2:
-        with jax.named_scope("gain2"):
-            gain_total = gain_total + lax.ppermute(gain_total, "seq", flips(2))
+    for flip_sets in ((4,), (8, 16, 24), (2, 32, 34)):
+        if max(flip_sets) < devices:
+            with jax.named_scope("gain" + str(flip_sets[0])):
+                terms = [lax.ppermute(gain_total, "seq", flips(flip)) for flip in flip_sets]
+            gain_total = gain_total + terms[0]
+            if len(terms) > 1:
+                gain_total = gain_total + (terms[1] + terms[2])
 
     bwd_two_part = after(bwd_two_part, fwd_two, gain_total)
 

time: 213 us -> 214 us (level)
  transfers between devices with their start and end apart: 19 -> 19, of which waited for: 10 -> 12; matrix products, arithmetic and copies ran while one was open for 10% -> 10% of each run, Pallas kernels for 16% -> 16%
where the time goes in v4:
time: 214 us; the launch traced here: 213 us
  waiting for transfers between devices  83.1 us (39%)
  starting transfers between devices  66.7 us (31%)
  Pallas kernels  36.3 us (17%)
  other arithmetic  15.2 us (7%)
  local copies, waits for them, and re-layouts  11 us (5%)
    ppermute x8, waiting for transfers between devices, swap(): return lax.ppermute(value, 'seq', flips(1))  55 us
    ppermute x8, starting transfers between devices, swap(): return lax.ppermute(value, 'seq', flips(1))  41.7 us
    ppermute x2, waiting for transfers between devices, shifted(): lax.ppermute(value, 'section', [(s, s + steps) for s in range(first, last)])  19.5 us
    pallas_call x2, Pallas kernels, backward(): pl.pallas_call(functools.partial(backward_body, STEP_HEADS), grid_spec=pl...  17.5 us
    ppermute x7, starting transfers between devices, on_device(): terms = [lax.ppermute(gain_total, 'seq', flips(flip)) for flip in flip_sets]  17.2 us
    pallas_call x2, Pallas kernels, forward(): pl.pallas_call(functools.partial(forward_body, query_rows, STEP_HEADS), g...  14.7 us
    ppermute x7, waiting for transfers between devices, on_device(): terms = [lax.ppermute(gain_total, 'seq', flips(flip)) for flip in flip_sets]  8.64 us
    reduce_sum x5, other arithmetic, inverse_norm(): return lax.rsqrt(jnp.mean(wide * wide, axis=1) + 1e-05)  7.58 us
  transfers between devices with their start and end apart: 19, of which 12 were waited for; matrix products, arithmetic and copies ran while one was open for 10% of the time, Pallas kernels for 16%

profile of v4, /device:TPU:32, one launch (start us, length us, event | category | flops | bytes accessed | tf_op | source)
XLA Modules:
  0.0 213.3 jit_solution(6276069687796470441)
XLA Ops:
  0.7 3.4 %collective-permute-start = (bf16[128,4096]{1,0:T(8,128)(2,1)}, bf16[128,4096]{1,0:T(8,128)(2,1)}, u32[]{:S(2)}, u32[]{:S(2)}) collective-permute-start(bf16[128,4096]{1,0:T(8,128)(2,1)} %bitcast.58), channel_id=1, source_target_pairs={{0,1},{1,0},{2,3},{3,2},{4,5},{5,4},{6,7},{7,6},{8,9},{9,8},{10,11... | collective-permute-start | bytes 3145736 | tf_op jit(solution)/shard_map/acts/ppermute | solution.py:326
  14.9 33.9 %collective-permute-done.other_ref = bf16[128,4096]{1,0:T(8,128)(2,1)} collective-permute-done((bf16[128,4096]{1,0:T(8,128)(2,1)}, bf16[128,4096]{1,0:T(8,128)(2,1)}, u32[]{:S(2)}, u32[]{:S(2)}) %collective-permute-start) | collective-permute-done | bytes 1048608 | tf_op jit(solution)/shard_map/acts/ppermute | solution.py:326
  48.8 26.5 %collective-permute-start.1 = (bf16[128,2176]{1,0:T(8,128)(2,1)S(1)}, bf16[128,2176]{1,0:T(8,128)(2,1)S(1)}, u32[]{:S(2)}, u32[]{:S(2)}) collective-permute-start(bf16[128,2176]{1,0:T(8,128)(2,1)S(1)} %fusion.2.inverse_own_ref), channel_id=1, source_target_pairs={{0,1},{1,0},{2,3},{3,2},{4,5},{5,4},{6,7},{7,6},{8,9},{9,8},{10,11... | collective-permute-start | bytes 1671176 | tf_op jit(solution)/shard_map/saved_a/ppermute | solution.py:326
  79.4 8.6 %attend256.1 = (bf16[128,4096]{1,0:T(8,128)(2,1)}, bf16[256,4096]{1,0:T(8,128)(2,1)}) custom-call(bf16[128,4096]{1,0:T(8,128)(2,1)S(1)} %bitcast.59, bf16[128,4096]{1,0:T(8,128)(2,1)} %collective-permute-done.other_ref, f32[2,128]{1,0:T(2,128)S(1)} %pad_maximum_fusion.inverse_ref, f32[3,4096]{1,0:T(4,128)S(1)} %bitcast.60, f32[1,32]{1,0:T(1,128)S(1)} %copy-done.13, ...), custom_call_target="tpu_custom_call" | custom-call | tf_op jit(solution)/shard_map/attend256/pallas_call | solution.py:96
  88.1 2.0 collective-permute-start.8
  90.1 4.3 %collective-permute-done.1.other_ref.inverse_other_ref = bf16[128,2176]{1,0:T(8,128)(2,1)S(1)} collective-permute-done((bf16[128,2176]{1,0:T(8,128)(2,1)S(1)}, bf16[128,2176]{1,0:T(8,128)(2,1)S(1)}, u32[]{:S(2)}, u32[]{:S(2)}) %collective-permute-start.1) | collective-permute-done | bytes 557088 | tf_op jit(solution)/shard_map/saved_a/ppermute | solution.py:326
  94.4 3.5 %collective-permute-start.4 = (bf16[128,2176]{1,0:T(8,128)(2,1)S(1)}, bf16[128,2176]{1,0:T(8,128)(2,1)S(1)}, u32[]{:S(2)}, u32[]{:S(2)}) collective-permute-start(bf16[128,2176]{1,0:T(8,128)(2,1)S(1)} %copy-done.4), channel_id=1, source_target_pairs={{0,1},{1,0},{2,3},{3,2},{4,5},{5,4},{6,7},{7,6},{8,9},{9,8},{10,11... | collective-permute-start | bytes 1671176 | tf_op jit(solution)/shard_map/saved_b/ppermute | solution.py:326
  99.4 6.3 %collective-permute-done.2.cot_other_ref = bf16[128,2048]{1,0:T(8,128)(2,1)S(1)} collective-permute-done((bf16[128,2048]{1,0:T(8,128)(2,1)}, bf16[128,2048]{1,0:T(8,128)(2,1)S(1)}, u32[]{:S(2)}, u32[]{:S(2)}) %collective-permute-start.2) | collective-permute-done | bytes 524320 | tf_op jit(solution)/shard_map/cot_a/ppermute | solution.py:326
  105.8 8.8 %differentiate.2 = (bf16[256,2048]{1,0:T(8,128)(2,1)S(1)}, f32[4,2048]{1,0:T(4,128)S(1)}) custom-call(s32[1]{0:T(128)} %bitcast.8.side_ref, bf16[128,4096]{1,0:T(8,128)(2,1)S(1)} %bitcast.52, bf16[128,2176]{1,0:T(8,128)(2,1)S(1)} %collective-permute-done.1.other_ref.inverse_other_ref, bf16[128,4096]{1,0:T(8,128)(2,1)S(1)} %bitcast.56, ...), custom_call_target="tpu_custom_call" | custom-call | tf_op jit(solution)/shard_map/differentiate/pallas_call | solution.py:201
  114.5 3.4 %collective-permute-start.3 = (f32[4,2048]{1,0:T(4,128)S(1)}, f32[4,2048]{1,0:T(4,128)S(1)}, u32[]{:S(2)}, u32[]{:S(2)}) collective-permute-start(f32[4,2048]{1,0:T(4,128)S(1)} %get-tuple-element.33.small_ref), channel_id=1, source_target_pairs={{0,1},{1,0},{2,3},{3,2},{4,5},{5,4},{6,7},{7,6},{8,9},{9,8},{10,11... | collective-permute-start | bytes 98312 | tf_op jit(solution)/shard_map/small_a/ppermute | solution.py:326
  118.0 6.7 %collective-permute-done.3.received_ref = f32[4,2048]{1,0:T(4,128)S(1)} collective-permute-done((f32[4,2048]{1,0:T(4,128)S(1)}, f32[4,2048]{1,0:T(4,128)S(1)}, u32[]{:S(2)}, u32[]{:S(2)}) %collective-permute-start.3) | collective-permute-done | bytes 32800 | tf_op jit(solution)/shard_map/small_a/ppermute | solution.py:326
  125.5 2.5 %combine.2 = (bf16[256,2048]{1,0:T(8,128)(2,1)}, bf16[128,2048]{1,0:T(8,128)(2,1)S(1)}) custom-call(s32[1]{0:T(128)} %bitcast.8.side_ref, bf16[128,4096]{1,0:T(8,128)(2,1)S(1)} %bitcast.53, bf16[128,2176]{1,0:T(8,128)(2,1)S(1)} %collective-permute-done.1.other_ref.inverse_other_ref, bf16[128,4096]{1,0:T(8,128)(2,1)S(1)} %bitcast.57, ...), custom_call_target="tpu_custom_call" | custom-call | tf_op jit(solution)/shard_map/combine/pallas_call | solution.py:268
  128.8 4.3 %collective-permute-start.7 = (bf16[256,2048]{1,0:T(8,128)(2,1)}, bf16[256,2048]{1,0:T(8,128)(2,1)}, u32[]{:S(2)}, u32[]{:S(2)}) collective-permute-start(bf16[256,2048]{1,0:T(8,128)(2,1)} %get-tuple-element.37), channel_id=1, source_target_pairs={{64,0},{128,64},{192,128},{65,1},{129,65},{193,129},{66,2},{130,66... | collective-permute-start | bytes 3145736 | tf_op jit(solution)/shard_map/to_previous/ppermute | solution.py:335
  134.4 19.5 %collective-permute-done.7 = bf16[256,2048]{1,0:T(8,128)(2,1)} collective-permute-done((bf16[256,2048]{1,0:T(8,128)(2,1)}, bf16[256,2048]{1,0:T(8,128)(2,1)}, u32[]{:S(2)}, u32[]{:S(2)}) %collective-permute-start.7) | collective-permute-done | bytes 1048608 | tf_op jit(solution)/shard_map/to_previous/ppermute | solution.py:335
  154.6 1.9 maximum_select_fusion.1.cot_own_ref.cot_other_ref
  156.6 8.7 %differentiate.3 = (bf16[256,2048]{1,0:T(8,128)(2,1)S(1)}, f32[4,2048]{1,0:T(4,128)S(1)}) custom-call(s32[1]{0:T(128)} %bitcast.8.side_ref, bf16[128,4096]{1,0:T(8,128)(2,1)S(1)} %bitcast.54, bf16[128,2176]{1,0:T(8,128)(2,1)S(1)} %collective-permute-done.4.other_ref.inverse_other_ref, bf16[256,2048]{1,0:T(8,128)(2,1)S(1)} %maximum_select_fusion.1.cot_own_ref.cot_other_ref, ...), custom_call_target="tpu_custom_call" | custom-call | tf_op jit(solution)/shard_map/differentiate/pallas_call | solution.py:201
  166.7 3.2 %collective-permute-done.6 = bf16[128,2048]{1,0:T(8,128)(2,1)S(1)} collective-permute-done((bf16[128,2048]{1,0:T(8,128)(2,1)}, bf16[128,2048]{1,0:T(8,128)(2,1)S(1)}, u32[]{:S(2)}, u32[]{:S(2)}) %collective-permute-start.6) | collective-permute-done | bytes 524320 | tf_op jit(solution)/shard_map/grad_one/ppermute | solution.py:326
  172.1 3.4 %collective-permute-start.11 = (bf16[128,2048]{1,0:T(8,128)(2,1)S(1)}, bf16[128,2048]{1,0:T(8,128)(2,1)S(1)}, u32[]{:S(2)}, u32[]{:S(2)}) collective-permute-start(bf16[128,2048]{1,0:T(8,128)(2,1)S(1)} %get-tuple-element.45), channel_id=1, source_target_pairs={{0,1},{1,0},{2,3},{3,2},{4,5},{5,4},{6,7},{7,6},{8,9},{9,8},{10,11... | collective-permute-start | bytes 1572872 | tf_op jit(solution)/shard_map/bwd_two/ppermute | solution.py:326
  180.0 3.8 %collective-permute-start.15 = (f32[3,4096]{1,0:T(4,128)S(1)}, f32[3,4096]{1,0:T(4,128)S(1)}, u32[]{:S(2)}, u32[]{:S(2)}) collective-permute-start(f32[3,4096]{1,0:T(4,128)S(1)} %add.138), channel_id=1, source_target_pairs={{0,24},{1,25},{2,26},{3,27},{4,28},{5,29},{6,30},{7,31},{8,16},{9,... | collective-permute-start | bytes 147464 | tf_op jit(solution)/shard_map/gain8/ppermute | solution.py:421
  185.0 2.6 %multiply_reduce_fusion = (f32[256]{0:T(256)S(1)}, bf16[256,4096]{1,0:T(8,128)(2,1)S(1)}) fusion(bf16[256,4096]{1,0:T(8,128)(2,1)} %collective-permute-done.8, bf16[128,4096]{1,0:T(8,128)(2,1)S(1)} %collective-permute-done.10, bf16[128,4096]{1,0:T(8,128)(2,1)S(1)} %copy-done.17, pred[]{:T(512)S(6)} %eq.15), kind=kLoop, calls=%fused_computation | loop fusion | flops 8388352 | bytes 6292481 | tf_op jit(solution)/shard_map/reduce_sum | solution.py:307
  188.0 2.0 collective-permute-done.13
  190.0 10.2 %collective-permute-start.18 = (f32[3,4096]{1,0:T(4,128)S(1)}, f32[3,4096]{1,0:T(4,128)S(1)}, u32[]{:S(2)}, u32[]{:S(2)}) collective-permute-start(f32[3,4096]{1,0:T(4,128)S(1)} %add_add_fusion.1), channel_id=1, source_target_pairs={{0,34},{1,35},{2,32},{3,33},{4,38},{5,39},{6,36},{7,37},{8,42},{9,... | collective-permute-start | bytes 147464 | tf_op jit(solution)/shard_map/gain2/ppermute | solution.py:421
  200.8 6.1 %attend128.1 = bf16[128,4096]{1,0:T(8,128)(2,1)} custom-call(bf16[256,4096]{1,0:T(8,128)(2,1)S(1)} %get-tuple-element.62.own_ref.other_ref, bf16[256,4096]{1,0:T(8,128)(2,1)S(1)} %get-tuple-element.62.own_ref.other_ref, f32[2,128]{1,0:T(2,128)S(1)} %rsqrt_bitcast_fusion.inverse_ref, f32[3,4096]{1,0:T(4,128)S(1)} %bitcast.63, f32[1,32]{1,0:T(1,128)S(1)} %copy-done.13, ...), custom_call_target="tpu_custom_call" | custom-call | tf_op jit(solution)/shard_map/attend128/pallas_call | solution.py:96
  206.9 3.1 %collective-permute-done.18 = f32[3,4096]{1,0:T(4,128)S(1)} collective-permute-done((f32[3,4096]{1,0:T(4,128)S(1)}, f32[3,4096]{1,0:T(4,128)S(1)}, u32[]{:S(2)}, u32[]{:S(2)}) %collective-permute-start.18) | collective-permute-done | bytes 49184 | tf_op jit(solution)/shard_map/gain2/ppermute | solution.py:421
  (102 shorter events, 33.7 us)
Async XLA Ops:
  0.7 48.2 %collective-permute-start = (bf16[128,4096]{1,0:T(8,128)(2,1)}, bf16[128,4096]{1,0:T(8,128)(2,1)}, u32[]{:S(2)}, u32[]{:S(2)}) collective-permute-start(bf16[128,4096]{1,0:T(8,128)(2,1)} %bitcast.58), channel_id=1, source_target_pairs={{0,1},{1,0},{2,3},{3,2},{4,5},{5,4},{6,7},{7,6},{8,9},{9,8},{10,11... | collective-permute-start | bytes 3145736 | tf_op jit(solution)/shard_map/acts/ppermute | solution.py:326
  9.2 66.1 %copy-start.19 = (f32[1,3,4096]{2,0,1:T(1,128)S(1)}, f32[1,3,4096]{2,0,1:T(1,128)}, u32[]{:S(2)}) copy-start(f32[1,3,4096]{2,0,1:T(1,128)} %param.16) | copy-start | bytes 147460
  11.9 65.3 %copy-start.13 = (f32[1,32]{1,0:T(1,128)S(1)}, f32[1,32]{1,0:T(1,128)}, u32[]{:S(2)}) copy-start(f32[1,32]{1,0:T(1,128)} %slopes_ref.7) | copy-start | bytes 388
  14.0 74.0 %copy-start.6 = (bf16[128,2176]{1,0:T(8,128)(2,1)}, bf16[128,2176]{1,0:T(8,128)(2,1)S(1)}, u32[]{:S(2)}) copy-start(bf16[128,2176]{1,0:T(8,128)(2,1)S(1)} %fusion.2.inverse_own_ref) | copy-start | bytes 1671172
  48.8 45.6 %collective-permute-start.1 = (bf16[128,2176]{1,0:T(8,128)(2,1)S(1)}, bf16[128,2176]{1,0:T(8,128)(2,1)S(1)}, u32[]{:S(2)}, u32[]{:S(2)}) collective-permute-start(bf16[128,2176]{1,0:T(8,128)(2,1)S(1)} %fusion.2.inverse_own_ref), channel_id=1, source_target_pairs={{0,1},{1,0},{2,3},{3,2},{4,5},{5,4},{6,7},{7,6},{8,9},{9,8},{10,11... | collective-permute-start | bytes 1671176 | tf_op jit(solution)/shard_map/saved_a/ppermute | solution.py:326
  75.5 30.2 %collective-permute-start.2 = (bf16[128,2048]{1,0:T(8,128)(2,1)}, bf16[128,2048]{1,0:T(8,128)(2,1)S(1)}, u32[]{:S(2)}, u32[]{:S(2)}) collective-permute-start(bf16[128,2048]{1,0:T(8,128)(2,1)} %dynamic-slice_bitcast_fusion.1), channel_id=1, source_target_pairs={{0,1},{1,0},{2,3},{3,2},{4,5},{5,4},{6,7},{7,6},{8,9},{9,8},{10,11... | collective-permute-start | bytes 1572872 | tf_op jit(solution)/shard_map/cot_a/ppermute | solution.py:326
  88.1 68.5 %collective-permute-start.8 = (bf16[256,4096]{1,0:T(8,128)(2,1)}, bf16[256,4096]{1,0:T(8,128)(2,1)}, u32[]{:S(2)}, u32[]{:S(2)}) collective-permute-start(bf16[256,4096]{1,0:T(8,128)(2,1)} %get-tuple-element.39), channel_id=1, source_target_pairs={{0,64},{64,128},{128,192},{1,65},{65,129},{129,193},{2,66},{66,130... | collective-permute-start | bytes 6291464 | tf_op jit(solution)/shard_map/to_next/ppermute | solution.py:335
  94.4 30.3 %collective-permute-start.4 = (bf16[128,2176]{1,0:T(8,128)(2,1)S(1)}, bf16[128,2176]{1,0:T(8,128)(2,1)S(1)}, u32[]{:S(2)}, u32[]{:S(2)}) collective-permute-start(bf16[128,2176]{1,0:T(8,128)(2,1)S(1)} %copy-done.4), channel_id=1, source_target_pairs={{0,1},{1,0},{2,3},{3,2},{4,5},{5,4},{6,7},{7,6},{8,9},{9,8},{10,11... | collective-permute-start | bytes 1671176 | tf_op jit(solution)/shard_map/saved_b/ppermute | solution.py:326
  98.7 25.9 %collective-permute-start.5 = (bf16[128,2048]{1,0:T(8,128)(2,1)S(1)}, bf16[128,2048]{1,0:T(8,128)(2,1)S(1)}, u32[]{:S(2)}, u32[]{:S(2)}) collective-permute-start(bf16[128,2048]{1,0:T(8,128)(2,1)S(1)} %get-tuple-element.35), channel_id=1, source_target_pairs={{192,193},{193,192},{194,195},{195,194},{196,197},{197,196},{198,1... | collective-permute-start | bytes 1572872 | tf_op jit(solution)/shard_map/cot_last/ppermute | solution.py:331
  114.5 10.1 %collective-permute-start.3 = (f32[4,2048]{1,0:T(4,128)S(1)}, f32[4,2048]{1,0:T(4,128)S(1)}, u32[]{:S(2)}, u32[]{:S(2)}) collective-permute-start(f32[4,2048]{1,0:T(4,128)S(1)} %get-tuple-element.33.small_ref), channel_id=1, source_target_pairs={{0,1},{1,0},{2,3},{3,2},{4,5},{5,4},{6,7},{7,6},{8,9},{9,8},{10,11... | collective-permute-start | bytes 98312 | tf_op jit(solution)/shard_map/small_a/ppermute | solution.py:326
  128.8 27.8 %copy-start.5 = (bf16[128,2176]{1,0:T(8,128)(2,1)S(1)}, bf16[128,2176]{1,0:T(8,128)(2,1)}, u32[]{:S(2)}) copy-start(bf16[128,2176]{1,0:T(8,128)(2,1)} %fusion.3.inverse_own_ref) | copy-start | bytes 1671172
  128.8 27.8 %copy-start.12 = (f32[256,256]{1,0:T(8,128)S(1)}, f32[256,256]{1,0:T(8,128)}, u32[]{:S(2)}) copy-start(f32[256,256]{1,0:T(8,128)} %get-tuple-element.69.table_ref) | copy-start | bytes 786436
  128.8 25.1 %collective-permute-start.7 = (bf16[256,2048]{1,0:T(8,128)(2,1)}, bf16[256,2048]{1,0:T(8,128)(2,1)}, u32[]{:S(2)}, u32[]{:S(2)}) collective-permute-start(bf16[256,2048]{1,0:T(8,128)(2,1)} %get-tuple-element.37), channel_id=1, source_target_pairs={{64,0},{128,64},{192,128},{65,1},{129,65},{193,129},{66,2},{130,66... | collective-permute-start | bytes 3145736 | tf_op jit(solution)/shard_map/to_previous/ppermute | solution.py:335
  133.2 36.7 %collective-permute-start.6 = (bf16[128,2048]{1,0:T(8,128)(2,1)}, bf16[128,2048]{1,0:T(8,128)(2,1)S(1)}, u32[]{:S(2)}, u32[]{:S(2)}) collective-permute-start(bf16[128,2048]{1,0:T(8,128)(2,1)} %copy-done.14), channel_id=1, source_target_pairs={{0,1},{1,0},{2,3},{3,2},{4,5},{5,4},{6,7},{7,6},{8,9},{9,8},{10,11... | collective-permute-start | bytes 1572872 | tf_op jit(solution)/shard_map/grad_one/ppermute | solution.py:326
  153.9 16.6 %collective-permute-start.10 = (bf16[128,4096]{1,0:T(8,128)(2,1)}, bf16[128,4096]{1,0:T(8,128)(2,1)S(1)}, u32[]{:S(2)}, u32[]{:S(2)}) collective-permute-start(bf16[128,4096]{1,0:T(8,128)(2,1)} %param.11), channel_id=1, source_target_pairs={{0,1},{1,0},{2,3},{3,2},{4,5},{5,4},{6,7},{7,6},{8,9},{9,8},{10,11... | collective-permute-start | bytes 3145736 | tf_op jit(solution)/shard_map/first_in/ppermute | solution.py:331
  165.4 5.1 %collective-permute-start.9 = (f32[4,2048]{1,0:T(4,128)S(1)}, f32[4,2048]{1,0:T(4,128)S(1)}, u32[]{:S(2)}, u32[]{:S(2)}) collective-permute-start(f32[4,2048]{1,0:T(4,128)S(1)} %select_add_fusion.small_ref), channel_id=1, source_target_pairs={{0,1},{1,0},{2,3},{3,2},{4,5},{5,4},{6,7},{7,6},{8,9},{9,8},{10,11... | collective-permute-start | bytes 98312 | tf_op jit(solution)/shard_map/small_b/ppermute | solution.py:326
  172.1 40.0 %collective-permute-start.11 = (bf16[128,2048]{1,0:T(8,128)(2,1)S(1)}, bf16[128,2048]{1,0:T(8,128)(2,1)S(1)}, u32[]{:S(2)}, u32[]{:S(2)}) collective-permute-start(bf16[128,2048]{1,0:T(8,128)(2,1)S(1)} %get-tuple-element.45), channel_id=1, source_target_pairs={{0,1},{1,0},{2,3},{3,2},{4,5},{5,4},{6,7},{7,6},{8,9},{9,8},{10,11... | collective-permute-start | bytes 1572872 | tf_op jit(solution)/shard_map/bwd_two/ppermute | solution.py:326
  175.6 4.4 %collective-permute-start.12 = (f32[3,4096]{1,0:T(4,128)S(1)}, f32[3,4096]{1,0:T(4,128)S(1)}, u32[]{:S(2)}, u32[]{:S(2)}) collective-permute-start(f32[3,4096]{1,0:T(4,128)S(1)} %maximum_select_fusion.4), channel_id=1, source_target_pairs={{0,4},{1,5},{2,6},{3,7},{4,0},{5,1},{6,2},{7,3},{8,12},{9,13},{10,... | collective-permute-start | bytes 147464 | tf_op jit(solution)/shard_map/gain4/ppermute | solution.py:421
  180.0 7.7 %collective-permute-start.15 = (f32[3,4096]{1,0:T(4,128)S(1)}, f32[3,4096]{1,0:T(4,128)S(1)}, u32[]{:S(2)}, u32[]{:S(2)}) collective-permute-start(f32[3,4096]{1,0:T(4,128)S(1)} %add.138), channel_id=1, source_target_pairs={{0,24},{1,25},{2,26},{3,27},{4,28},{5,29},{6,30},{7,31},{8,16},{9,... | collective-permute-start | bytes 147464 | tf_op jit(solution)/shard_map/gain8/ppermute | solution.py:421
  183.7 4.3 %collective-permute-start.14 = (f32[3,4096]{1,0:T(4,128)S(1)}, f32[3,4096]{1,0:T(4,128)S(1)}, u32[]{:S(2)}, u32[]{:S(2)}) collective-permute-start(f32[3,4096]{1,0:T(4,128)S(1)} %add.138), channel_id=1, source_target_pairs={{0,16},{1,17},{2,18},{3,19},{4,20},{5,21},{6,22},{7,23},{8,24},{9,... | collective-permute-start | bytes 147464 | tf_op jit(solution)/shard_map/gain8/ppermute | solution.py:421
  184.2 5.8 %collective-permute-start.13 = (f32[3,4096]{1,0:T(4,128)S(1)}, f32[3,4096]{1,0:T(4,128)S(1)}, u32[]{:S(2)}, u32[]{:S(2)}) collective-permute-start(f32[3,4096]{1,0:T(4,128)S(1)} %add.138), channel_id=1, source_target_pairs={{0,8},{1,9},{2,10},{3,11},{4,12},{5,13},{6,14},{7,15},{8,0},{9,1},... | collective-permute-start | bytes 147464 | tf_op jit(solution)/shard_map/gain8/ppermute | solution.py:421
  190.0 20.0 %collective-permute-start.18 = (f32[3,4096]{1,0:T(4,128)S(1)}, f32[3,4096]{1,0:T(4,128)S(1)}, u32[]{:S(2)}, u32[]{:S(2)}) collective-permute-start(f32[3,4096]{1,0:T(4,128)S(1)} %add_add_fusion.1), channel_id=1, source_target_pairs={{0,34},{1,35},{2,32},{3,33},{4,38},{5,39},{6,36},{7,37},{8,42},{9,... | collective-permute-start | bytes 147464 | tf_op jit(solution)/shard_map/gain2/ppermute | solution.py:421
  200.2 9.9 %collective-permute-start.17 = (f32[3,4096]{1,0:T(4,128)S(1)}, f32[3,4096]{1,0:T(4,128)S(1)}, u32[]{:S(2)}, u32[]{:S(2)}) collective-permute-start(f32[3,4096]{1,0:T(4,128)S(1)} %add_add_fusion.1), channel_id=1, source_target_pairs={{0,32},{1,33},{2,34},{3,35},{4,36},{5,37},{6,38},{7,39},{8,40},{9,... | collective-permute-start | bytes 147464 | tf_op jit(solution)/shard_map/gain2/ppermute | solution.py:421
  200.5 10.8 %collective-permute-start.16 = (f32[3,4096]{1,0:T(4,128)S(1)}, f32[3,4096]{1,0:T(4,128)S(1)}, u32[]{:S(2)}, u32[]{:S(2)}) collective-permute-start(f32[3,4096]{1,0:T(4,128)S(1)} %add_add_fusion.1), channel_id=1, source_target_pairs={{0,2},{1,3},{2,0},{3,1},{4,6},{5,7},{6,4},{7,5},{8,10},{9,11},{10,... | collective-permute-start | bytes 147464 | tf_op jit(solution)/shard_map/gain2/ppermute | solution.py:421
  (15 other events, 167.1 us)
